TPU v7x, 32 devices: a whole 2x2x4 slice. The times are simulated.
32 devices in a mesh: row: 4 (over z), col: 8 (over y, x, core).
Axes of the slice: x: 2, y: 2, z: 4, core: 2. Of those that a mesh axis runs over, the one named last changes fastest.
Arguments:
- right_side: float32 [8, 16384], P(None, ('row', 'col')), may hold values from -30 to 30
- u_factors: bfloat16 [32, 64, 48, 512], P(('row', 'col')), may hold values from -0.109375 to 0.109375
- v_factors: bfloat16 [32, 64, 48, 512], P('row', 'col'), may hold values from -0.25 to 0.25
- ranks: int32 [32, 64], P('row', 'col'), may hold values from 8 to 48
- far_blocks: bfloat16 [8, 512, 32768], P('row', None, 'col'), may hold values from -0.09375 to 0.09375
- block_target: int32 [8, 8], replicated, may hold values from 0 to 31, as said below
- recv_order: int32 [32], replicated, may hold values from 0 to 31, as said below
Outputs:
- densities: float32 [8, 32768], P(None, 'col')
- residual: float32 [8, 16384], P(None, ('row', 'col'))
- far_field: float32 [32, 4096], P(('row', 'col'))
Inputs may be any that keep to these rules, and one draw needn't show every extreme that they name: `recv_order`: a permutation of the receiver patches. `block_target`: block (b, c) with b % 2 == 0 lies on device g = (b // 2) * 8 + c; its receiver patch is stored in output rows owned by device (g + 32 / 2) mod 32 if g is even and by device g - 1 if g is odd; the other blocks may name any receiver patch.
All inputs are finite; a program needn't handle non-finite values.
Results may differ from a plain program's by a relative error of at most 0.008.
Values may be sent and summed in bfloat16 or wider, within the bound.
A program may use at most 128 MiB of HBM per device.

v0:
```python
import jax
import jax.numpy as jnp
from jax import lax
from jax.sharding import PartitionSpec as P

ITERS = 2


def per_device(right_side, u_factors, v_factors, ranks, far_blocks, block_target, recv_order):
    dens_count = right_side.shape[0]
    own_rows = u_factors.shape[0]
    all_cols = u_factors.shape[1]
    slot_count = u_factors.shape[2]
    patch_len = u_factors.shape[3]
    group_rows = v_factors.shape[0]
    own_cols = v_factors.shape[1]
    slot_index = lax.broadcasted_iota(jnp.int32, (group_rows, own_cols, slot_count, 1), 2)
    kept = (slot_index < ranks[:, :, None, None]).astype(jnp.float32)
    kept_half = kept.astype(jnp.bfloat16)
    residual = right_side
    densities = jnp.zeros((dens_count, own_cols * patch_len), jnp.float32)
    for iteration in range(ITERS):
        res_bf = residual.astype(jnp.bfloat16).reshape(dens_count, own_rows, patch_len)
        back_coef = jnp.einsum(
            "ijsp,dip->ijsd", u_factors, res_bf, preferred_element_type=jnp.float32
        )
        back_coef = back_coef.astype(jnp.bfloat16).reshape(
            own_rows, all_cols, slot_count * dens_count
        )
        arrived = lax.all_to_all(back_coef, "col", split_axis=1, concat_axis=0, tiled=True)
        arrived = arrived.reshape(group_rows, own_cols, slot_count, dens_count) * kept_half
        partial_grad = jnp.einsum(
            "ijsp,ijsd->djp", v_factors, arrived, preferred_element_type=jnp.float32
        )
        grad = lax.psum(partial_grad.reshape(dens_count, own_cols * patch_len), "row")
        grad_local = jnp.sum(grad * grad, axis=1)
        grad_sq = lax.psum(grad_local, "col")
        grad_bf = grad.astype(jnp.bfloat16).reshape(dens_count, own_cols, patch_len)
        coefficients = (
            jnp.einsum("ijsp,djp->ijsd", v_factors, grad_bf, preferred_element_type=jnp.float32)
            * kept
        )
        coefficients = coefficients.astype(jnp.bfloat16).reshape(
            group_rows, own_cols, slot_count * dens_count
        )
        landed = lax.all_to_all(coefficients, "col", split_axis=0, concat_axis=1, tiled=True)
        landed = landed.reshape(own_rows, all_cols, slot_count, dens_count)
        image = jnp.einsum("ijsp,ijsd->dip", u_factors, landed, preferred_element_type=jnp.float32)
        image = image.reshape(dens_count, own_rows * patch_len)
        image_local = jnp.sum(image * image, axis=1)
        image_sq = lax.psum(image_local, ("row", "col"))
        step_size = grad_sq / (image_sq + 1e-06)
        densities = densities + step_size[:, None] * grad
        residual = residual - step_size[:, None] * image
    block_count = far_blocks.shape[0]
    x_half = densities.astype(jnp.bfloat16)
    block_field = jnp.einsum("bpn,dn->bdp", far_blocks, x_half, preferred_element_type=jnp.float32)
    block_field = block_field.reshape(block_count, dens_count * patch_len)
    row_count = lax.axis_size("row")
    col_count = lax.axis_size("col")
    device_count = row_count * col_count
    recv_total = recv_order.shape[0]
    mine_count = recv_total // device_count
    local_target = lax.dynamic_slice(
        block_target, (lax.axis_index("row") * block_count, lax.axis_index("col")), (block_count, 1)
    ).reshape(block_count)
    recv_iota = lax.broadcasted_iota(jnp.int32, (block_count, recv_total), 1)
    matches = local_target[:, None] == recv_order[None, :]
    position = jnp.sum(jnp.where(matches, recv_iota, 0), axis=1)
    owner = position // mine_count
    slot_row = (position % mine_count).astype(jnp.float32)
    device_iota = lax.broadcasted_iota(jnp.int32, (device_count, block_count), 0)
    owner_mask = device_iota == owner[None, :]
    send_fields = jnp.where(owner_mask[:, :, None], block_field[None, :, :], 0.0)
    send_rows = jnp.where(owner_mask, slot_row[None, :], -1.0)
    got_fields, got_rows = (
        lax.all_to_all(
            send_fields.astype(jnp.bfloat16),
            ("row", "col"),
            split_axis=0,
            concat_axis=0,
            tiled=True,
        ).astype(send_fields.dtype),
        lax.all_to_all(
            send_rows.astype(jnp.bfloat16), ("row", "col"), split_axis=0, concat_axis=0, tiled=True
        ).astype(send_rows.dtype),
    )
    got_fields = got_fields.reshape(device_count * block_count, dens_count * patch_len)
    got_rows = got_rows.reshape(device_count * block_count)
    mine_iota = lax.broadcasted_iota(jnp.int32, (device_count * block_count, mine_count), 1).astype(
        jnp.float32
    )
    placing = (got_rows[:, None] == mine_iota).astype(jnp.float32)
    far_field = jnp.dot(
        placing.T, got_fields, preferred_element_type=jnp.float32, precision=lax.Precision.HIGHEST
    )
    return (densities, residual, far_field)


def solution(mesh):
    return jax.shard_map(
        per_device,
        mesh=mesh,
        in_specs=(
            P(None, ("row", "col")),
            P(("row", "col"), None, None, None),
            P("row", "col", None, None),
            P("row", "col"),
            P("row", None, "col"),
            P(),
            P(),
        ),
        out_specs=(P(None, "col"), P(None, ("row", "col")), P(("row", "col"), None)),
        check_vma=False,
    )
```

profile of v0, /device:TPU:0, one launch (start us, length us, event | category | flops | bytes accessed | tf_op | source)
XLA Modules:
  0.0 301.9 jit_solution(16736316005141044228)
XLA Ops:
  7.2 1.9 copy-done
  9.1 2.3 convolution_convert_fusion
  11.4 0.2 copy.50
  11.5 0.2 copy.51
  11.7 0.5 broadcast.118
  12.2 0.9 reduce.8
  13.1 0.6 reshape.207
  13.8 5.2 %all-to-all-start = ((bf16[8,2,1536]{2,1,0:T(2,128)(2,1)}), bf16[8,2,1536]{2,1,0:T(2,128)(2,1)S(1)}, u32[]{:S(2)}, u32[]{:S(2)}) async-start(bf16[8,2,1536]{2,1,0:T(2,128)(2,1)} %reshape.207), calls=%async_computation | async-start | bytes 98304 | tf_op jit(solution)/shard_map/all_to_all | solution.py:30
  18.9 0.0 all-reduce.3.cloned.1.call-start
  19.0 0.1 copy.52
  19.1 0.1 fusion.38
  19.2 4.7 %all-to-all-done = bf16[8,2,1536]{2,1,0:T(2,128)(2,1)S(1)} async-done(((bf16[8,2,1536]{2,1,0:T(2,128)(2,1)}), bf16[8,2,1536]{2,1,0:T(2,128)(2,1)S(1)}, u32[]{:S(2)}, u32[]{:S(2)}) %all-to-all-start) | async-done | bytes 49184 | tf_op jit(solution)/shard_map/all_to_all | solution.py:30
  23.9 0.3 bitcast_reduce_fusion.1
  24.2 1.8 reshape.179
  26.0 3.8 %fusion.32 = f32[8,8,512,1]{2,1,0,3:T(8,128)} fusion(bf16[8,8,48,512]{3,2,1,0:T(8,128)(2,1)} %param.9, bf16[8,8,48,8]{3,2,1,0:T(8,128)(2,1)} %reshape.179, bf16[8,8,48]{2,1,0:T(8,128)(2,1)S(1)} %copy.53), kind=kOutput, calls=%fused_computation.21 | convolution fusion | flops 25190400 | bytes 3332096 | tf_op jit(solution)/shard_map/ijsp,ijsd->djp/dot_general | solution.py:32
  29.8 0.0 all-reduce.3.cloned.1.call-update
  29.8 34.0 %all-reduce.3.cloned.1.call-done = f32[8,4096]{1,0:T(8,128)} async-done(((f32[8,4096]{1,0:T(8,128)}), f32[8,4096]{1,0:T(8,128)}) %all-reduce.3.cloned.1.call-update) | async-done | bytes 131088 | tf_op jit(solution)/shard_map/psum | solution.py:35
  63.8 1.1 multiply_reduce_fusion.1
  64.9 3.5 %fusion.18 = bf16[8,8,48,8]{2,3,0,1:T(8,128)(2,1)S(1)} fusion(bf16[8,8,512,1]{2,0,3,1:T(8,128)(2,1)S(1)} %bitcast.91, bf16[8,8,48,512]{3,2,1,0:T(8,128)(2,1)} %param.9, f32[8,8,48]{2,0,1:T(8,128)S(1)} %get-tuple-element.7), kind=kOutput, calls=%fused_computation.11 | convolution fusion | flops 25214976 | bytes 3272704 | tf_op jit(solution)/shard_map/ijsp,djp->ijsd/dot_general | solution.py:40
  68.4 1.2 copy.56
  69.6 2.5 reshape.182
  72.1 3.6 %all-to-all-start.1 = ((bf16[8,8,384]{2,1,0:T(8,128)(2,1)}), bf16[8,8,384]{2,1,0:T(8,128)(2,1)S(1)}, u32[]{:S(2)}, u32[]{:S(2)}) async-start(bf16[8,8,384]{2,1,0:T(8,128)(2,1)} %reshape.182), calls=%async_computation.1 | async-start | bytes 98304 | tf_op jit(solution)/shard_map/all_to_all | solution.py:46
  75.7 0.9 dynamic-slice_reduce_fusion
  76.6 14.5 %psum.43 = f32[8]{0:T(128)S(1)} all-reduce(f32[8]{0:T(128)S(1)} %get-tuple-element.5), channel_id=1, replica_groups=mesh['row'=4,'col'=8] {'col'}, use_global_device_ids=true, to_apply=%region_2.0 | all-reduce | flops 8 | bytes 64 | tf_op jit(solution)/shard_map/psum | solution.py:37
  91.1 1.8 reshape.183
  92.9 1.8 multiply_reduce_fusion.3
  94.7 39.2 %psum.44 = f32[8]{0:T(128)S(1)} all-reduce(f32[8]{0:T(128)S(1)} %get-tuple-element.9), channel_id=1, replica_groups=mesh['row'=4,'col'=8] {'row','col'}, use_global_device_ids=true, to_apply=%region_4.0 | all-reduce | flops 8 | bytes 64 | tf_op jit(solution)/shard_map/psum | solution.py:51
  133.9 0.6 copy-done.9
  134.5 3.4 %fusion.27 = bf16[1,64,384]{1,2,0:T(8,128)(2,1)S(1)} fusion(bf16[64,48,512]{2,1,0:T(8,128)(2,1)S(1)} %bitcast.85, f32[8,512]{1,0:T(8,128)S(1)} %copy-done.4, f32[8,512]{1,0:T(8,128)S(1)} %get-tuple-element.10, f32[8]{0:T(128)S(1)} %add_divide_fusion.1), kind=kOutput, calls=%fused_computation.14 | convolution fusion | flops 25202688 | bytes 3227680 | tf_op jit(solution)/shard_map/ijsp,dip->ijsd/dot_general | solution.py:24
  137.9 0.2 copy.59
  138.0 0.9 reduce.9
  139.0 0.6 reshape.209
  139.6 3.6 %all-to-all-start.2 = ((bf16[8,2,1536]{2,1,0:T(2,128)(2,1)}), bf16[8,2,1536]{2,1,0:T(2,128)(2,1)S(1)}, u32[]{:S(2)}, u32[]{:S(2)}) async-start(bf16[8,2,1536]{2,1,0:T(2,128)(2,1)} %reshape.209), calls=%async_computation.2 | async-start | bytes 98304 | tf_op jit(solution)/shard_map/all_to_all | solution.py:30
  143.2 0.2 all-reduce.5.cloned.1.call-start
  143.4 0.2 fusion.45
  143.6 4.5 %all-to-all-done.2 = bf16[8,2,1536]{2,1,0:T(2,128)(2,1)S(1)} async-done(((bf16[8,2,1536]{2,1,0:T(2,128)(2,1)}), bf16[8,2,1536]{2,1,0:T(2,128)(2,1)S(1)}, u32[]{:S(2)}, u32[]{:S(2)}) %all-to-all-start.2) | async-done | bytes 49184 | tf_op jit(solution)/shard_map/all_to_all | solution.py:30
  148.1 0.3 bitcast_reduce_fusion
  148.4 1.8 reshape.185
  150.2 3.8 %fusion.30 = f32[8,8,512,1]{2,1,0,3:T(8,128)} fusion(bf16[8,8,48,512]{3,2,1,0:T(8,128)(2,1)} %param.9, bf16[8,8,48,8]{3,2,1,0:T(8,128)(2,1)} %reshape.185, bf16[8,8,48]{2,1,0:T(8,128)(2,1)S(1)} %copy.53), kind=kOutput, calls=%fused_computation.19 | convolution fusion | flops 25190400 | bytes 3332096 | tf_op jit(solution)/shard_map/ijsp,ijsd->djp/dot_general | solution.py:32
  154.0 0.0 all-reduce.5.cloned.1.call-update
  154.0 0.6 fusion.39
  154.7 31.9 %all-reduce.5.cloned.1.call-done = f32[8,4096]{1,0:T(8,128)} async-done(((f32[8,4096]{1,0:T(8,128)}), f32[8,4096]{1,0:T(8,128)}) %all-reduce.5.cloned.1.call-update) | async-done | bytes 131088 | tf_op jit(solution)/shard_map/psum | solution.py:35
  186.6 1.6 fusion.49
  188.2 3.5 %fusion.21 = bf16[8,8,48,8]{2,3,0,1:T(8,128)(2,1)S(1)} fusion(bf16[8,8,512,1]{2,0,3,1:T(8,128)(2,1)S(1)} %bitcast.92, bf16[8,8,48,512]{3,2,1,0:T(8,128)(2,1)} %param.9, f32[8,8,48]{2,0,1:T(8,128)S(1)} %get-tuple-element.7), kind=kOutput, calls=%fused_computation.12 | convolution fusion | flops 25214976 | bytes 3272704 | tf_op jit(solution)/shard_map/ijsp,djp->ijsd/dot_general | solution.py:40
  191.7 1.2 copy.62
  192.9 2.5 reshape.188
  195.4 3.6 %all-to-all-start.3 = ((bf16[8,8,384]{2,1,0:T(8,128)(2,1)}), bf16[8,8,384]{2,1,0:T(8,128)(2,1)S(1)}, u32[]{:S(2)}, u32[]{:S(2)}) async-start(bf16[8,8,384]{2,1,0:T(8,128)(2,1)} %reshape.188), calls=%async_computation.3 | async-start | bytes 98304 | tf_op jit(solution)/shard_map/all_to_all | solution.py:46
  199.0 1.2 iota_compare_fusion.1
  200.2 14.6 %psum.46 = f32[8]{0:T(128)S(1)} all-reduce(f32[8]{0:T(128)} %get-tuple-element.4), channel_id=1, replica_groups=mesh['row'=4,'col'=8] {'col'}, use_global_device_ids=true, to_apply=%region_7.0 | all-reduce | flops 8 | bytes 64 | tf_op jit(solution)/shard_map/psum | solution.py:37
  214.8 3.2 %all-to-all-start.4 = ((bf16[32,1,2]{2,1,0:T(2,128)(2,1)}), bf16[32,1,2]{2,1,0:T(2,128)(2,1)}, u32[]{:S(2)}, u32[]{:S(2)}) async-start(bf16[32,1,2]{2,1,0:T(2,128)(2,1)} %fusion.39), calls=%async_computation.4 | async-start | bytes 32768 | tf_op jit(solution)/shard_map/all_to_all | solution.py:84
  218.0 1.8 reshape.189
  219.8 2.4 multiply_reduce_fusion.2
  222.2 40.4 %psum.47 = f32[8]{0:T(128)S(1)} all-reduce(f32[8]{0:T(128)S(1)} %get-tuple-element.11), channel_id=1, replica_groups=mesh['row'=4,'col'=8] {'row','col'}, use_global_device_ids=true, to_apply=%region_9.0 | all-reduce | flops 8 | bytes 64 | tf_op jit(solution)/shard_map/psum | solution.py:51
  262.6 0.5 copy-done.12
  263.1 0.8 multiply_add_fusion
  263.9 5.7 %convolution_bitcast_fusion = bf16[1,2,8,512]{3,2,1,0:T(8,128)(2,1)S(1)} fusion(bf16[2,512,4096]{2,1,0:T(8,128)(2,1)} %param.11, f32[8,4096]{1,0:T(8,128)S(1)} %multiply_add_fusion), kind=kOutput, calls=%fused_computation.15 | convolution fusion | flops 67141632 | bytes 8536064 | tf_op jit(solution)/shard_map/bpn,dn->bdp/dot_general | solution.py:57
  269.7 1.4 select_convert_fusion
  271.1 4.6 %all-to-all-start.5 = ((bf16[32,2,4096]{2,1,0:T(2,128)(2,1)}), bf16[32,2,4096]{2,1,0:T(2,128)(2,1)}, u32[]{:S(2)}, u32[]{:S(2)}) async-start(bf16[32,2,4096]{2,1,0:T(2,128)(2,1)} %select_convert_fusion), calls=%async_computation.5 | async-start | bytes 1048576 | tf_op jit(solution)/shard_map/all_to_all | solution.py:77
  275.7 0.8 compare_reduce_fusion
  276.5 0.1 reshape.200
  276.6 0.7 multiply_subtract_fusion
  277.3 13.9 %all-to-all-done.5 = bf16[32,2,4096]{2,1,0:T(2,128)(2,1)} async-done(((bf16[32,2,4096]{2,1,0:T(2,128)(2,1)}), bf16[32,2,4096]{2,1,0:T(2,128)(2,1)}, u32[]{:S(2)}, u32[]{:S(2)}) %all-to-all-start.5) | async-done | bytes 524320 | tf_op jit(solution)/shard_map/all_to_all | solution.py:77
  291.2 2.0 reshape.190
  293.3 1.8 fusion.50
  (38 shorter events, 0.2 us)
Async XLA Ops:
  7.2 1.9 copy-start
  7.2 11.8 %copy-start.11 = (s32[8,8]{1,0:T(8,128)S(1)}, s32[8,8]{1,0:T(8,128)}, u32[]{:S(2)}) copy-start(s32[8,8]{1,0:T(8,128)} %param.10) | copy-start | bytes 772
  13.8 10.1 %all-to-all-start = ((bf16[8,2,1536]{2,1,0:T(2,128)(2,1)}), bf16[8,2,1536]{2,1,0:T(2,128)(2,1)S(1)}, u32[]{:S(2)}, u32[]{:S(2)}) async-start(bf16[8,2,1536]{2,1,0:T(2,128)(2,1)} %reshape.207), calls=%async_computation | async-start | bytes 98304 | tf_op jit(solution)/shard_map/all_to_all | solution.py:30
  18.9 44.9 %all-reduce.3.cloned.1.call-start = ((), (), s32[]{:S(2)}) async-start(), calls=%async_computation.6 | async-start | bytes 262144 | tf_op jit(solution)/shard_map/psum | solution.py:35
  68.4 66.1 %copy-start.4 = (f32[8,512]{1,0:T(8,128)S(1)}, f32[8,512]{1,0:T(8,128)}, u32[]{:S(2)}) copy-start(f32[8,512]{1,0:T(8,128)} %param.7) | copy-start | bytes 49156
  72.1 18.9 %all-to-all-start.1 = ((bf16[8,8,384]{2,1,0:T(8,128)(2,1)}), bf16[8,8,384]{2,1,0:T(8,128)(2,1)S(1)}, u32[]{:S(2)}, u32[]{:S(2)}) async-start(bf16[8,8,384]{2,1,0:T(8,128)(2,1)} %reshape.182), calls=%async_computation.1 | async-start | bytes 98304 | tf_op jit(solution)/shard_map/all_to_all | solution.py:46
  92.9 50.5 %copy-start.15 = (s32[32]{0:T(128)S(1)}, s32[32]{0:T(128)}, u32[]{:S(2)}) copy-start(s32[32]{0:T(128)} %param.13) | copy-start | bytes 388
  94.7 39.2 %copy-start.5 = (f32[8,512]{1,0:T(8,128)}, f32[8,512]{1,0:T(8,128)S(1)}, u32[]{:S(2)}) copy-start(f32[8,512]{1,0:T(8,128)S(1)} %get-tuple-element.10) | copy-start | bytes 49156
  133.9 0.6 copy-start.9
  139.6 8.5 %all-to-all-start.2 = ((bf16[8,2,1536]{2,1,0:T(2,128)(2,1)}), bf16[8,2,1536]{2,1,0:T(2,128)(2,1)S(1)}, u32[]{:S(2)}, u32[]{:S(2)}) async-start(bf16[8,2,1536]{2,1,0:T(2,128)(2,1)} %reshape.209), calls=%async_computation.2 | async-start | bytes 98304 | tf_op jit(solution)/shard_map/all_to_all | solution.py:30
  143.2 43.4 %all-reduce.5.cloned.1.call-start = ((), (), s32[]{:S(2)}) async-start(), calls=%async_computation.7 | async-start | bytes 262144 | tf_op jit(solution)/shard_map/psum | solution.py:35
  143.6 11.1 %copy-start.14 = (s32[2]{0:T(128)}, s32[2]{0:T(128)S(1)}, u32[]{:S(2)}) copy-start(s32[2]{0:T(128)S(1)} %fusion.45) | copy-start | bytes 28
  191.7 71.4 %copy-start.2 = (f32[8,4096]{1,0:T(8,128)S(1)}, f32[8,4096]{1,0:T(8,128)}, u32[]{:S(2)}) copy-start(f32[8,4096]{1,0:T(8,128)} %all-reduce.3.cloned.1.call-done) | copy-start | bytes 393220
  191.7 71.4 %copy-start.3 = (f32[8,4096]{1,0:T(8,128)S(1)}, f32[8,4096]{1,0:T(8,128)}, u32[]{:S(2)}) copy-start(f32[8,4096]{1,0:T(8,128)} %all-reduce.5.cloned.1.call-done) | copy-start | bytes 393220
  195.4 19.4 %all-to-all-start.3 = ((bf16[8,8,384]{2,1,0:T(8,128)(2,1)}), bf16[8,8,384]{2,1,0:T(8,128)(2,1)S(1)}, u32[]{:S(2)}, u32[]{:S(2)}) async-start(bf16[8,8,384]{2,1,0:T(8,128)(2,1)} %reshape.188), calls=%async_computation.3 | async-start | bytes 98304 | tf_op jit(solution)/shard_map/all_to_all | solution.py:46
  214.8 56.3 %all-to-all-start.4 = ((bf16[32,1,2]{2,1,0:T(2,128)(2,1)}), bf16[32,1,2]{2,1,0:T(2,128)(2,1)}, u32[]{:S(2)}, u32[]{:S(2)}) async-start(bf16[32,1,2]{2,1,0:T(2,128)(2,1)} %fusion.39), calls=%async_computation.4 | async-start | bytes 32768 | tf_op jit(solution)/shard_map/all_to_all | solution.py:84
  262.6 0.5 copy-start.12
  263.9 5.8 %copy-start.1 = (f32[8,4096]{1,0:T(8,128)}, f32[8,4096]{1,0:T(8,128)S(1)}, u32[]{:S(2)}) copy-start(f32[8,4096]{1,0:T(8,128)S(1)} %multiply_add_fusion) | copy-start | bytes 393220
  263.9 5.8 %copy-start.8 = (pred[32,2]{1,0:T(8,128)(4,1)S(1)}, pred[32,2]{1,0:T(8,128)(4,1)}, u32[]{:S(2)}) copy-start(pred[32,2]{1,0:T(8,128)(4,1)} %iota_compare_fusion.1) | copy-start | bytes 196
  263.9 12.7 %copy-start.6 = (f32[8,512]{1,0:T(8,128)S(1)}, f32[8,512]{1,0:T(8,128)}, u32[]{:S(2)}) copy-start(f32[8,512]{1,0:T(8,128)} %copy-done.5) | copy-start | bytes 49156
  263.9 12.7 %copy-start.7 = (f32[8,512]{1,0:T(8,128)S(1)}, f32[8,512]{1,0:T(8,128)}, u32[]{:S(2)}) copy-start(f32[8,512]{1,0:T(8,128)} %get-tuple-element.12) | copy-start | bytes 49156
  263.9 12.7 %copy-start.10 = (f32[8]{0:T(128)S(1)}, f32[8]{0:T(128)}, u32[]{:S(2)}) copy-start(f32[8]{0:T(128)} %copy-done.9) | copy-start | bytes 100
  263.9 12.7 %copy-start.13 = (f32[8]{0:T(128)S(1)}, f32[8]{0:T(128)}, u32[]{:S(2)}) copy-start(f32[8]{0:T(128)} %copy-done.12) | copy-start | bytes 100
  271.1 20.1 %all-to-all-start.5 = ((bf16[32,2,4096]{2,1,0:T(2,128)(2,1)}), bf16[32,2,4096]{2,1,0:T(2,128)(2,1)}, u32[]{:S(2)}, u32[]{:S(2)}) async-start(bf16[32,2,4096]{2,1,0:T(2,128)(2,1)} %select_convert_fusion), calls=%async_computation.5 | async-start | bytes 1048576 | tf_op jit(solution)/shard_map/all_to_all | solution.py:77
Sparse Core Ops, SparseCore 0:
  29.9 33.8 all-reduce.2
  154.2 32.3 all-reduce.4
where the time goes:
time: 303 us; the launch traced here: 302 us
  blocking collectives  109 us (36%)
  waiting for transfers between devices  89.1 us (29%)
  matrix products  32 us (11%)
  starting transfers between devices  24 us (8%)
  local copies, waits for them, and re-layouts  23.6 us (8%)
  between operations  14.3 us (5%)
  other arithmetic  10.3 us (3%)
    psum x2, blocking collectives, per_device(): image_sq = lax.psum(image_local, ('row', 'col'))  79.7 us
    psum x2, waiting for transfers between devices, per_device(): lax.psum(partial_grad.reshape(dens_count, own_cols * patch_len), 'row')  65.9 us
    psum x2, blocking collectives, per_device(): grad_sq = lax.psum(grad_local, 'col')  29 us
    all_to_all x1, waiting for transfers between devices, per_device(): lax.all_to_all(send_fields.astype(jnp.bfloat16), ('row', 'col'), split_ax...  13.9 us
    all_to_all x2, waiting for transfers between devices, per_device(): lax.all_to_all(back_coef, 'col', split_axis=1, concat_axis=0, tiled=True)  9.23 us
    all_to_all x2, starting transfers between devices, per_device(): lax.all_to_all(back_coef, 'col', split_axis=1, concat_axis=0, tiled=True)  8.72 us
    dot_general x2, matrix products, per_device(): jnp.einsum('ijsp,ijsd->djp', v_factors, arrived, preferred_element_type=j...  7.65 us
    all_to_all x2, starting transfers between devices, per_device(): lax.all_to_all(coefficients, 'col', split_axis=0, concat_axis=1, tiled=True)  7.21 us
  transfers between devices with their start and end apart: 8, of which 5 were waited for; matrix products, arithmetic and copies ran while one was open for 6% of the time, Pallas kernels for 0%

commit v1 on v0

v1 whole, which is shorter than its diff:
```python
import functools

import jax
import jax.numpy as jnp
from jax import lax
from jax.experimental import pallas as pl
from jax.experimental.pallas import tpu as pltpu
from jax.sharding import PartitionSpec as P

MESH = pl.DeviceIdType.MESH
LANES = 128
NT = (((1,), (1,)), ((), ()))
NN = (((1,), (0,)), ((), ()))


def partner_of(me, k, n):
    if n & (n - 1):
        return (me + k) % n
    out = 0
    bit = 1
    while bit < n:
        mine = (me // bit) % 2
        out = out + bit * ((1 - mine) if k & bit else mine)
        bit *= 2
    return out


def sender_to(me, k, n):
    if n & (n - 1):
        return (me + n - k) % n
    return partner_of(me, k, n)


def kernel(
    nr, nc, dens_count, own_cols, slot_count, patch,
    rhs_ref, ranks_ref, target_ref, order_ref, u_hbm, v_hbm, f_hbm,
    dens_ref, resid_ref, far_ref,
    u_v, v_v, f_v, kept_ref, acc_ref, sum_ref,
    a2a_out, a2a_in, rs_out, rs_in, ag_buf, sc_col, sc_row, z_buf, fc_out, fc_in, ev_out, ev_in,
    u_sem, v_sem, f_sem, a2a_ss, a2a_rs, rs_ss, rs_rs, ag_ss, ag_rs,
    scc_ss, scc_rs, scr_ss, scr_rs, z_ss, z_rs, fc_ss, fc_rs, ev_ss, ev_rs,
):
    d = dens_count
    slots = own_cols * slot_count
    half = a2a_out.shape[-1]
    rows = own_cols * d
    chunk = rows // nr
    my_r = lax.axis_index("row")
    my_c = lax.axis_index("col")
    far_first = list(range(nc - 1, 0, -1))
    near_first = list(range(1, nc))
    row_first = list(range(nr - 1, 0, -1))
    bf = jnp.bfloat16
    f32 = jnp.float32

    u_copies = {}
    v_copies = {}
    for k in far_first + [0]:
        to = partner_of(my_c, k, nc)
        u_copies[k] = pltpu.make_async_copy(u_hbm.at[to], u_v.at[to], u_sem.at[k])
        u_copies[k].start()
    for k in [0] + near_first:
        frm = sender_to(my_c, k, nc)
        v_copies[k] = pltpu.make_async_copy(v_hbm.at[frm], v_v.at[frm], v_sem.at[k])
        v_copies[k].start()
    f_copies = []
    for b in range(2):
        f_copies.append(pltpu.make_async_copy(f_hbm.at[b], f_v.at[b], f_sem.at[b]))
        f_copies[b].start()

    barrier = pltpu.get_barrier_semaphore()
    for k in near_first:
        pl.semaphore_signal(
            barrier, inc=1, device_id=(my_r, partner_of(my_c, k, nc)), device_id_type=MESH
        )
    for k in row_first:
        pl.semaphore_signal(
            barrier, inc=1, device_id=(partner_of(my_r, k, nr), my_c), device_id_type=MESH
        )

    pending = []

    def send(src, dst, ssem, rsem, r, c):
        copy = pltpu.make_async_remote_copy(
            src_ref=src, dst_ref=dst, send_sem=ssem, recv_sem=rsem,
            device_id=(r, c), device_id_type=MESH,
        )
        copy.start()
        pending.append(copy)

    def arrive(src, dst, ssem, rsem):
        pltpu.make_async_remote_copy(
            src_ref=src, dst_ref=dst, send_sem=ssem, recv_sem=rsem,
            device_id=(my_r, my_c), device_id_type=MESH,
        ).wait_recv()

    def pack(x):
        top, low = x[:, :half], x[:, half:]
        if low.shape[1] < half:
            low = jnp.concatenate([low, jnp.zeros((d, half - low.shape[1]), f32)], axis=1)
        return jnp.concatenate([top, low], axis=0).astype(bf)

    def unpack(x):
        x = x.astype(f32)
        return jnp.concatenate([x[:d], x[d:, : slots - half]], axis=1)

    def post(rnd, to, k, value):
        if k == 0:
            a2a_in[rnd, my_c] = pack(value)
            return
        a2a_out[rnd, to] = pack(value)
        send(
            a2a_out.at[rnd, to], a2a_in.at[rnd, my_c], a2a_ss.at[rnd, to], a2a_rs.at[rnd, my_c],
            my_r, to,
        )

    def take(rnd, frm, k):
        if k:
            arrive(
                a2a_out.at[rnd, frm], a2a_in.at[rnd, frm], a2a_ss.at[rnd, frm],
                a2a_rs.at[rnd, frm],
            )
        return unpack(a2a_in[rnd, frm])

    lane_col = lax.broadcasted_iota(jnp.int32, (d, slots), 1) // slot_count
    diag = jnp.concatenate(
        [(lane_col == j).astype(f32) for j in range(own_cols)], axis=0
    )

    def back_pass(rnd, r, first):
        rb = r.astype(bf)
        for k in far_first + [0]:
            to = partner_of(my_c, k, nc)
            if first:
                u_copies[k].wait()
            value = lax.dot_general(rb, u_v[to], NT, preferred_element_type=f32)
            if first and k == far_first[0]:
                pl.semaphore_wait(barrier, nc - 1 + nr - 1)
            post(rnd, to, k, value)

    def grad_pass(rnd, first):
        acc = jnp.zeros((rows, patch), f32)
        for k in [0] + near_first:
            frm = sender_to(my_c, k, nc)
            if first:
                v_copies[k].wait()
            b = take(rnd, frm, k) * kept_ref[pl.ds(frm, 1), :]
            wide = (jnp.concatenate([b] * own_cols, axis=0) * diag).astype(bf)
            acc = acc + lax.dot_general(wide, v_v[frm], NN, preferred_element_type=f32)
        return acc

    def row_reduce(it, acc):
        acc_ref[...] = acc.reshape(nr, chunk, patch)
        for k in row_first:
            to = partner_of(my_r, k, nr)
            rs_out[it, to] = acc_ref[to].astype(rs_out.dtype)
            send(
                rs_out.at[it, to], rs_in.at[it, my_r], rs_ss.at[it, to], rs_rs.at[it, my_r],
                to, my_c,
            )
        total = acc_ref[my_r]
        for k in row_first[::-1]:
            frm = sender_to(my_r, k, nr)
            arrive(
                rs_out.at[it, frm], rs_in.at[it, frm], rs_ss.at[it, frm], rs_rs.at[it, frm]
            )
            total = total + rs_in[it, frm].astype(f32)
        return total

    def row_gather(it, g):
        ag_buf[it, my_r] = g.astype(ag_buf.dtype)
        for k in row_first:
            to = partner_of(my_r, k, nr)
            send(
                ag_buf.at[it, my_r], ag_buf.at[it, my_r], ag_ss.at[it, to], ag_rs.at[it, my_r],
                to, my_c,
            )
        for k in row_first[::-1]:
            frm = sender_to(my_r, k, nr)
            arrive(
                ag_buf.at[it, frm], ag_buf.at[it, frm], ag_ss.at[it, frm], ag_rs.at[it, frm]
            )
        return ag_buf[it].reshape(rows, patch).astype(bf)

    def coef_pass(rnd, g):
        for k in far_first + [0]:
            to = partner_of(my_c, k, nc)
            wide = lax.dot_general(g, v_v[to], NT, preferred_element_type=f32) * diag
            c = wide[:d]
            for j in range(1, own_cols):
                c = c + wide[j * d : (j + 1) * d]
            post(rnd, to, k, c * kept_ref[pl.ds(to, 1), :])

    def image_pass(rnd):
        image = jnp.zeros((d, patch), f32)
        for k in [0] + near_first:
            frm = sender_to(my_c, k, nc)
            c = take(rnd, frm, k).astype(bf)
            image = image + lax.dot_general(c, u_v[frm], NN, preferred_element_type=f32)
        return image

    lane = lax.broadcasted_iota(jnp.int32, (d, LANES), 1)

    def squares_out(it, g, image):
        grad_sq = jnp.zeros((d, 1), f32)
        for j in range(chunk // d):
            part = g[j * d : (j + 1) * d]
            grad_sq = grad_sq + jnp.sum(part * part, axis=1, keepdims=True)
        image_sq = jnp.sum(image * image, axis=1, keepdims=True)
        sc_col[it, my_c] = jnp.where(lane < LANES // 2, grad_sq, image_sq)
        for k in far_first:
            to = partner_of(my_c, k, nc)
            send(
                sc_col.at[it, my_c], sc_col.at[it, my_c], scc_ss.at[it, to],
                scc_rs.at[it, my_c], my_r, to,
            )

    def squares_on(it):
        for k in near_first:
            frm = sender_to(my_c, k, nc)
            arrive(
                sc_col.at[it, frm], sc_col.at[it, frm], scc_ss.at[it, frm], scc_rs.at[it, frm]
            )
        total = sc_col[it, 0]
        for c in range(1, nc):
            total = total + sc_col[it, c]
        sc_row[it, my_r] = total
        for k in row_first:
            to = partner_of(my_r, k, nr)
            send(
                sc_row.at[it, my_r], sc_row.at[it, my_r], scr_ss.at[it, to],
                scr_rs.at[it, my_r], to, my_c,
            )

    def squares_in(it):
        for k in row_first[::-1]:
            frm = sender_to(my_r, k, nr)
            arrive(
                sc_row.at[it, frm], sc_row.at[it, frm], scr_ss.at[it, frm], scr_rs.at[it, frm]
            )
        total = sc_row[it, 0]
        for r in range(1, nr):
            total = total + sc_row[it, r]
        return total[:, :1] / (total[:, LANES // 2 : LANES // 2 + 1] + 1e-6)

    rhs = rhs_ref[...]
    back_pass(0, rhs, True)
    lane_all = lax.broadcasted_iota(jnp.int32, (nc, slots), 1)
    ranks = ranks_ref[...]
    limit = jnp.zeros((nc, slots), jnp.int32)
    for j in range(own_cols):
        limit = jnp.where(lane_all // slot_count == j, ranks[:, j : j + 1], limit)
    kept_ref[...] = (lane_all % slot_count < limit).astype(f32)

    g1 = row_reduce(0, grad_pass(0, True))
    g1_all = row_gather(0, g1)
    coef_pass(1, g1_all)
    image1 = image_pass(1)
    back_pass(2, image1, False)
    squares_out(0, g1, image1)
    squares_on(0)
    h1 = row_reduce(1, grad_pass(2, False))
    step1 = squares_in(0)

    g2 = g1 - jnp.concatenate([step1] * (chunk // d), axis=0) * h1
    g2_all = row_gather(1, g2)
    coef_pass(3, g2_all)

    g1_wide = g1_all.astype(f32)
    g2_wide = g2_all.astype(f32)

    def field_of(b):
        f_copies[b].wait()
        field = jnp.zeros((2 * d, patch), f32)
        for j in range(own_cols):
            lhs = jnp.concatenate(
                [g1_wide[j * d : (j + 1) * d], g2_wide[j * d : (j + 1) * d]], axis=0
            ).astype(bf)
            field = field + lax.dot_general(
                lhs, f_v[b, :, j * patch : (j + 1) * patch], NT, preferred_element_type=f32
            )
        return field.astype(bf)

    z_buf[my_r] = field_of(1)
    for k in row_first:
        to = partner_of(my_r, k, nr)
        send(z_buf.at[my_r], z_buf.at[my_r], z_ss.at[to], z_rs.at[my_r], to, my_c)
    ev_out[...] = field_of(0)
    odd = my_c % 2
    ev_row = (1 - odd) * ((my_r + nr // 2) % nr) + odd * my_r
    ev_col = my_c - odd
    send(ev_out, ev_in.at[odd], ev_ss, ev_rs.at[odd], ev_row, ev_col)

    image2 = image_pass(3)
    squares_out(1, g2, image2)

    for k in row_first[::-1]:
        frm = sender_to(my_r, k, nr)
        arrive(z_buf.at[frm], z_buf.at[frm], z_ss.at[frm], z_rs.at[frm])
    fields = [z_buf[r].astype(f32) for r in range(nr)]
    targets = [target_ref[2 * r + 1, my_c] for r in range(nr)]
    for k in far_first + [0]:
        to = partner_of(my_c, k, nc)
        wanted = order_ref[my_r * nc + to]
        part = jnp.zeros((2 * d, patch), f32)
        for r in range(nr):
            part = part + fields[r] * jnp.where(targets[r] == wanted, 1.0, 0.0).astype(f32)
        if k:
            fc_out[to] = part.astype(bf)
            send(fc_out.at[to], fc_in.at[my_c], fc_ss.at[to], fc_rs.at[my_c], my_r, to)
        else:
            fc_in[my_c] = part.astype(bf)

    squares_on(1)
    for k in near_first:
        frm = sender_to(my_c, k, nc)
        arrive(fc_out.at[frm], fc_in.at[frm], fc_ss.at[frm], fc_rs.at[frm])
    got = fc_in[0].astype(f32)
    for c in range(1, nc):
        got = got + fc_in[c].astype(f32)

    sum_ref[...] = got

    @pl.when(odd == 0)
    def _():
        for s in range(2):
            arrive(ev_out, ev_in.at[s], ev_ss, ev_rs.at[s])
        sum_ref[...] = got + ev_in[0].astype(f32) + ev_in[1].astype(f32)

    field = sum_ref[...]
    step2 = squares_in(1)
    far = step1 * field[:d] + step2 * field[d:]
    for row in range(d):
        far_ref[:, row * patch : (row + 1) * patch] = far[row : row + 1]
    resid_ref[...] = rhs - step1 * image1 - step2 * image2
    for j in range(own_cols):
        dens_ref[:, j * patch : (j + 1) * patch] = (
            step1 * g1_wide[j * d : (j + 1) * d] + step2 * g2_wide[j * d : (j + 1) * d]
        )
    for copy in pending:
        copy.wait_send()


def per_device(nr, nc, right_side, u_factors, v_factors, ranks, far_blocks, block_target, recv_order):
    dens_count, patch = right_side.shape
    own_rows, all_cols, slot_count, _ = u_factors.shape
    group_rows, own_cols = v_factors.shape[:2]
    block_count, _, unknowns = far_blocks.shape
    recv_total = recv_order.shape[0]
    assert own_rows == 1 and group_rows == nc and all_cols == nc * own_cols
    assert block_count == 2 and recv_total == nr * nc and unknowns == own_cols * patch
    slots = own_cols * slot_count
    rows = own_cols * dens_count
    chunk = rows // nr
    half = -(-slots // (2 * LANES)) * LANES
    bf = jnp.bfloat16
    f32 = jnp.float32
    wire = bf if chunk % 16 == 0 else f32
    dma = pltpu.SemaphoreType.DMA
    u = u_factors.reshape(nc, slots, patch)
    v = v_factors.reshape(group_rows, slots, patch)
    vmem = pl.BlockSpec(memory_space=pltpu.VMEM)
    smem = pl.BlockSpec(memory_space=pltpu.SMEM)
    hbm = pl.BlockSpec(memory_space=pl.ANY)
    scratch = [
        pltpu.VMEM(u.shape, bf),
        pltpu.VMEM(v.shape, bf),
        pltpu.VMEM(far_blocks.shape, bf),
        pltpu.VMEM((nc, slots), f32),
        pltpu.VMEM((nr, chunk, patch), f32),
        pltpu.VMEM((2 * dens_count, patch), f32),
        pltpu.VMEM((4, nc, 2 * dens_count, half), bf),
        pltpu.VMEM((4, nc, 2 * dens_count, half), bf),
        pltpu.VMEM((2, nr, chunk, patch), wire),
        pltpu.VMEM((2, nr, chunk, patch), wire),
        pltpu.VMEM((2, nr, chunk, patch), wire),
        pltpu.VMEM((2, nc, dens_count, LANES), f32),
        pltpu.VMEM((2, nr, dens_count, LANES), f32),
        pltpu.VMEM((nr, 2 * dens_count, patch), bf),
        pltpu.VMEM((nc, 2 * dens_count, patch), bf),
        pltpu.VMEM((nc, 2 * dens_count, patch), bf),
        pltpu.VMEM((2 * dens_count, patch), bf),
        pltpu.VMEM((2, 2 * dens_count, patch), bf),
        dma((nc,)), dma((nc,)), dma((2,)),
        dma((4, nc)), dma((4, nc)),
        dma((2, nr)), dma((2, nr)),
        dma((2, nr)), dma((2, nr)),
        dma((2, nc)), dma((2, nc)),
        dma((2, nr)), dma((2, nr)),
        dma((nr,)), dma((nr,)),
        dma((nc,)), dma((nc,)),
        dma, dma((2,)),
    ]
    matrix = u.size + v.size
    return pl.pallas_call(
        functools.partial(kernel, nr, nc, dens_count, own_cols, slot_count, patch),
        out_shape=(
            jax.ShapeDtypeStruct((dens_count, unknowns), f32),
            jax.ShapeDtypeStruct((dens_count, patch), f32),
            jax.ShapeDtypeStruct((1, dens_count * patch), f32),
        ),
        in_specs=[vmem, vmem, smem, smem, hbm, hbm, hbm],
        out_specs=(vmem, vmem, vmem),
        scratch_shapes=scratch,
        compiler_params=pltpu.CompilerParams(
            collective_id=0, has_side_effects=True, vmem_limit_bytes=56 * 1024 * 1024
        ),
        cost_estimate=pl.CostEstimate(
            flops=8 * dens_count * matrix + 2 * dens_count * far_blocks.size,
            bytes_accessed=2 * (matrix + far_blocks.size), transcendentals=0,
        ),
    )(right_side, ranks, block_target, recv_order, u, v, far_blocks)


def solution(mesh):
    return jax.shard_map(
        functools.partial(per_device, mesh.shape["row"], mesh.shape["col"]),
        mesh=mesh,
        in_specs=(
            P(None, ("row", "col")),
            P(("row", "col"), None, None, None),
            P("row", "col", None, None),
            P("row", "col"),
            P("row", None, "col"),
            P(),
            P(),
        ),
        out_specs=(P(None, "col"), P(None, ("row", "col")), P(("row", "col"), None)),
        check_vma=False,
    )
```

time: 303 us -> 57.6 us (0.19)
  blocking collectives: 109 us -> 0 us
  waiting for transfers between devices: 89.1 us -> 0 us
  Pallas kernels: 0 us -> 52.3 us
  matrix products: 32 us -> 0 us
  starting transfers between devices: 24 us -> 0 us
  local copies, waits for them, and re-layouts: 23.6 us -> 4.21 us
  between operations: 14.3 us -> 0.64 us
  other arithmetic: 10.3 us -> 0 us
    psum x4 -> x0, blocking collectives: 109 us -> none  [the longest x2 79.7 us: per_device(): image_sq = lax.psum(image_local, ('row', 'col'))]
    psum x2 -> x0, waiting for transfers between devices: 65.9 us -> none  [per_device(): lax.psum(partial_grad.reshape(dens_count, own_cols * patch_len), 'row')]
    pallas_call x0 -> x1, Pallas kernels: none -> 52.3 us  [per_device(): pl.pallas_call(functools.partial(kernel, nr, nc, dens_count, own_cols, sl...]
    dot_general x10 -> x0, matrix products: 32 us -> none  [the longest x2 7.65 us: per_device(): jnp.einsum('ijsp,ijsd->djp', v_factors, arrived, preferred_element_type=j...]
    all_to_all x6 -> x0, starting transfers between devices: 23.7 us -> none  [the longest x2 8.72 us: per_device(): lax.all_to_all(back_coef, 'col', split_axis=1, concat_axis=0, tiled=True)]
    all_to_all x6 -> x0, waiting for transfers between devices: 23.1 us -> none  [the longest x1 13.9 us: per_device(): lax.all_to_all(send_fields.astype(jnp.bfloat16), ('row', 'col'), split_ax...]
    reshape x7 -> x0, local copies, waits for them, and re-layouts: 11 us -> none  [the longest x2 5.02 us: per_device(): coefficients.astype(jnp.bfloat16)]
    convert_element_type x4 -> x0, other arithmetic: 3.75 us -> none  [the longest x1 1.63 us: per_device(): grad_bf = grad.astype(jnp.bfloat16).reshape(dens_count, own_cols, patch_len)]
  transfers between devices with their start and end apart: 8 -> 0, of which waited for: 5 -> 0; matrix products, arithmetic and copies ran while one was open for 6% -> 0% of each run, Pallas kernels for 0% -> 0%
where the time goes in v1:
time: 57.6 us; the launch traced here: 57.1 us
  Pallas kernels  52.3 us (91%)
  local copies, waits for them, and re-layouts  4.21 us (7%)
  between operations  0.64 us (1%)
    pallas_call x1, Pallas kernels, per_device(): pl.pallas_call(functools.partial(kernel, nr, nc, dens_count, own_cols, sl...  52.3 us
    unnamed x3, local copies, waits for them, and re-layouts  4.21 us

profile of v1, /device:TPU:0, one launch (start us, length us, event | category | flops | bytes accessed | tf_op | source)
XLA Modules:
  0.0 57.1 jit_solution(15509742541500747443)
XLA Ops:
  0.6 52.3 %shard_map.94 = (f32[8,4096]{1,0:T(8,128)}, f32[8,512]{1,0:T(8,128)}, f32[1,4096]{1,0:T(1,128)}) custom-call(f32[8,512]{1,0:T(8,128)} %rhs_ref.1, s32[8,8]{1,0:T(8,128)} %ranks_ref.1, s32[8,8]{1,0:T(8,128)} %target_ref.1, s32[32]{0:T(128)} %order_ref.1, bf16[8,384,512]{2,1,0:T(8,128)(2,1)} %bitcast.2, bf16[8,384,512]{2,1,0:T(8,128)(2,1)} %bitcast.3, ...), custom_call_target="tpu_custom_call" | custom-call | flops 268435456 | bytes 14680064 | tf_op jit(solution)/shard_map/pallas_call | solution.py:395
  52.9 1.6 %copy.13 = f32[8,4096]{1,0:T(8,128)} copy(f32[8,4096]{1,0:T(8,128)} %get-tuple-element.6) | data formatting | bytes 262144
  54.5 1.3 %copy.14 = f32[8,512]{1,0:T(8,128)} copy(f32[8,512]{1,0:T(8,128)} %get-tuple-element.7) | data formatting | bytes 32768
  55.8 1.3 %copy.15 = f32[1,4096]{1,0:T(1,128)} copy(f32[1,4096]{1,0:T(1,128)} %get-tuple-element.8) | data formatting | bytes 32768

commit v2 on v1

v2 whole, which is shorter than its diff:
```python
import functools

import jax
import jax.numpy as jnp
from jax import lax
from jax.experimental import pallas as pl
from jax.experimental.pallas import tpu as pltpu
from jax.sharding import PartitionSpec as P

MESH = pl.DeviceIdType.MESH
LANES = 128
NT = (((1,), (1,)), ((), ()))
NN = (((1,), (0,)), ((), ()))


def partner_of(me, k, n):
    if n & (n - 1):
        return (me + k) % n
    out = 0
    bit = 1
    while bit < n:
        mine = (me // bit) % 2
        out = out + bit * ((1 - mine) if k & bit else mine)
        bit *= 2
    return out


def kernel(
    nr, nc, dens_count, own_cols, slot_count, patch,
    rhs_ref, ranks_ref, target_ref, order_ref, u_hbm, v_hbm, f_hbm,
    dens_ref, resid_ref, far_ref,
    u_v, v_v, f_v, kept_ref, acc_ref, sum_ref,
    a2a_out, a2a_in, rs_out, rs_in, ag_buf, sc_col, sc_row, z_buf, fc_out, fc_in, ev_out, ev_in,
    load_sem, a2a_ss, a2a_rs, rs_ss, rs_rs, ag_ss, ag_rs,
    scc_ss, scc_rs, scr_ss, scr_rs, z_ss, z_rs, fc_ss, fc_rs, ev_ss, ev_rs,
):
    d = dens_count
    slots = own_cols * slot_count
    half = a2a_out.shape[-1]
    rows = own_cols * d
    chunk = rows // nr
    my_r = lax.axis_index("row")
    my_c = lax.axis_index("col")
    col_peers = [partner_of(my_c, k, nc) for k in range(nc - 1, 0, -1)]
    row_peers = [partner_of(my_r, k, nr) for k in range(nr - 1, 0, -1)]
    bf = jnp.bfloat16
    f32 = jnp.float32

    u_copy = pltpu.make_async_copy(u_hbm, u_v, load_sem.at[0])
    v_copy = pltpu.make_async_copy(v_hbm, v_v, load_sem.at[1])
    f_copies = [pltpu.make_async_copy(f_hbm.at[b], f_v.at[b], load_sem.at[2 + b]) for b in range(2)]
    u_copy.start()

    barrier = pltpu.get_barrier_semaphore()
    for to in col_peers:
        pl.semaphore_signal(barrier, inc=1, device_id=(my_r, to), device_id_type=MESH)
    for to in row_peers:
        pl.semaphore_signal(barrier, inc=1, device_id=(to, my_c), device_id_type=MESH)

    def remote(src, dst, ssem, rsem, r, c):
        return pltpu.make_async_remote_copy(
            src_ref=src, dst_ref=dst, send_sem=ssem, recv_sem=rsem,
            device_id=(r, c), device_id_type=MESH,
        )

    def over_col(out, into, ssem, rsem, shared=False):
        for to in col_peers:
            src = out.at[my_c] if shared else out.at[to]
            remote(src, into.at[my_c], ssem, rsem, my_r, to).start()
        return remote(out.at[: nc - 1], into.at[: nc - 1], ssem, rsem, my_r, my_c)

    def over_row(out, into, ssem, rsem, shared=False):
        for to in row_peers:
            src = out.at[my_r] if shared else out.at[to]
            remote(src, into.at[my_r], ssem, rsem, to, my_c).start()
        return remote(out.at[: nr - 1], into.at[: nr - 1], ssem, rsem, my_r, my_c)

    def pack(x):
        top, low = x[:, :half], x[:, half:]
        if low.shape[1] < half:
            low = jnp.concatenate([low, jnp.zeros((d, half - low.shape[1]), f32)], axis=1)
        return jnp.concatenate([top, low], axis=0).astype(bf)

    def unpack(x):
        x = x.astype(f32)
        return jnp.concatenate([x[:d], x[d:, : slots - half]], axis=1)

    def exchange(rnd, values):
        for c in range(nc):
            a2a_out[rnd, c] = pack(values[c])
        sent = over_col(a2a_out.at[rnd], a2a_in.at[rnd], a2a_ss.at[rnd], a2a_rs.at[rnd])
        a2a_in[rnd, my_c] = a2a_out[rnd, my_c]
        return sent

    lane_col = lax.broadcasted_iota(jnp.int32, (d, slots), 1) // slot_count
    diag = jnp.concatenate([(lane_col == j).astype(f32) for j in range(own_cols)], axis=0)

    def back_of(r):
        rb = r.astype(bf)
        return [
            lax.dot_general(rb, u_v[c], NT, preferred_element_type=f32) for c in range(nc)
        ]

    def grad_of(rnd):
        acc = jnp.zeros((rows, patch), f32)
        for c in range(nc):
            b = unpack(a2a_in[rnd, c]) * kept_ref[c : c + 1, :]
            wide = (jnp.concatenate([b] * own_cols, axis=0) * diag).astype(bf)
            acc = acc + lax.dot_general(wide, v_v[c], NN, preferred_element_type=f32)
        return acc.reshape(nr, chunk, patch)

    def reduce_start(it, acc):
        rs_out[it] = acc.astype(rs_out.dtype)
        sent = over_row(rs_out.at[it], rs_in.at[it], rs_ss.at[it], rs_rs.at[it])
        acc_ref[...] = acc
        rs_in[it, my_r] = jnp.zeros((chunk, patch), rs_in.dtype)
        return sent

    def reduce_end(it, sent):
        total = acc_ref[my_r]
        sent.wait_recv()
        for r in range(nr):
            total = total + rs_in[it, r].astype(f32)
        return total

    def gather_start(it, g):
        ag_buf[it, my_r] = g.astype(ag_buf.dtype)
        return over_row(ag_buf.at[it], ag_buf.at[it], ag_ss.at[it], ag_rs.at[it], shared=True)

    def gathered(it):
        return ag_buf[it].reshape(rows, patch).astype(bf)

    def coef_of(g):
        values = []
        for c in range(nc):
            wide = lax.dot_general(g, v_v[c], NT, preferred_element_type=f32) * diag
            part = wide[:d]
            for j in range(1, own_cols):
                part = part + wide[j * d : (j + 1) * d]
            values.append(part * kept_ref[c : c + 1, :])
        return values

    def image_of(rnd):
        image = jnp.zeros((d, patch), f32)
        for c in range(nc):
            coef = unpack(a2a_in[rnd, c]).astype(bf)
            image = image + lax.dot_general(coef, u_v[c], NN, preferred_element_type=f32)
        return image

    lane = lax.broadcasted_iota(jnp.int32, (d, LANES), 1)

    def squares_out(it, g, image):
        squares = jnp.zeros((d, patch), f32)
        for j in range(chunk // d):
            squares = squares + g[j * d : (j + 1) * d] * g[j * d : (j + 1) * d]
        grad_sq = jnp.sum(squares, axis=1, keepdims=True)
        image_sq = jnp.sum(image * image, axis=1, keepdims=True)
        sc_col[it, my_c] = jnp.where(lane < LANES // 2, grad_sq, image_sq)
        return over_col(
            sc_col.at[it], sc_col.at[it], scc_ss.at[it], scc_rs.at[it], shared=True
        )

    def squares_on(it, sent):
        sent.wait_recv()
        total = sc_col[it, 0]
        for c in range(1, nc):
            total = total + sc_col[it, c]
        sc_row[it, my_r] = total
        return over_row(
            sc_row.at[it], sc_row.at[it], scr_ss.at[it], scr_rs.at[it], shared=True
        )

    def squares_in(it, sent):
        sent.wait_recv()
        total = sc_row[it, 0]
        for r in range(1, nr):
            total = total + sc_row[it, r]
        return total[:, :1] / (total[:, LANES // 2 : LANES // 2 + 1] + 1e-6)

    rhs = rhs_ref[...]
    lane_all = lax.broadcasted_iota(jnp.int32, (nc, slots), 1)
    ranks = ranks_ref[...]
    limit = jnp.zeros((nc, slots), jnp.int32)
    for j in range(own_cols):
        limit = jnp.where(lane_all // slot_count == j, ranks[:, j : j + 1], limit)
    kept_ref[...] = (lane_all % slot_count < limit).astype(f32)
    u_copy.wait()
    v_copy.start()
    back0 = back_of(rhs)
    pl.semaphore_wait(barrier, nc - 1 + nr - 1)
    x0 = exchange(0, back0)
    v_copy.wait()
    for copy in f_copies[::-1]:
        copy.start()
    x0.wait_recv()
    s0 = reduce_start(0, grad_of(0))
    x0.wait_send()
    g1 = reduce_end(0, s0)
    a0 = gather_start(0, g1)
    s0.wait_send()
    a0.wait_recv()
    g1_all = gathered(0)
    x1 = exchange(1, coef_of(g1_all))
    a0.wait_send()
    x1.wait_recv()
    image1 = image_of(1)
    x2 = exchange(2, back_of(image1))
    q0 = squares_out(0, g1, image1)
    x1.wait_send()
    x2.wait_recv()
    s1 = reduce_start(1, grad_of(2))
    p0 = squares_on(0, q0)
    x2.wait_send()
    h1 = reduce_end(1, s1)
    step1 = squares_in(0, p0)

    g2 = g1 - jnp.concatenate([step1] * (chunk // d), axis=0) * h1
    a1 = gather_start(1, g2)
    s1.wait_send()
    q0.wait_send()
    p0.wait_send()
    a1.wait_recv()
    g2_all = gathered(1)
    x3 = exchange(3, coef_of(g2_all))

    g1_wide = g1_all.astype(f32)
    g2_wide = g2_all.astype(f32)

    def field_of(b):
        field = jnp.zeros((2 * d, patch), f32)
        for j in range(own_cols):
            lhs = jnp.concatenate(
                [g1_wide[j * d : (j + 1) * d], g2_wide[j * d : (j + 1) * d]], axis=0
            ).astype(bf)
            field = field + lax.dot_general(
                lhs, f_v[b, :, j * patch : (j + 1) * patch], NT, preferred_element_type=f32
            )
        return field.astype(bf)

    for copy in f_copies:
        copy.wait()
    z_buf[my_r] = field_of(1)
    z = over_row(z_buf, z_buf, z_ss, z_rs, shared=True)
    x3.wait_recv()
    image2 = image_of(3)
    q1 = squares_out(1, g2, image2)

    ev_out[...] = field_of(0)
    odd = my_c % 2
    ev_row = (1 - odd) * ((my_r + nr // 2) % nr) + odd * my_r
    ev = remote(ev_out, ev_in.at[odd], ev_ss, ev_rs.at[odd], ev_row, my_c - odd)
    ev.start()
    p1 = squares_on(1, q1)

    z.wait_recv()
    fields = [z_buf[r].astype(f32) for r in range(nr)]
    targets = [target_ref[2 * r + 1, my_c] for r in range(nr)]
    for to in range(nc):
        wanted = order_ref[my_r * nc + to]
        part = jnp.zeros((2 * d, patch), f32)
        for r in range(nr):
            part = part + fields[r] * jnp.where(targets[r] == wanted, 1.0, 0.0).astype(f32)
        fc_out[to] = part.astype(bf)
    fc = over_col(fc_out, fc_in, fc_ss, fc_rs)
    fc_in[my_c] = fc_out[my_c]
    x3.wait_send()
    a1.wait_send()
    z.wait_send()
    q1.wait_send()
    step2 = squares_in(1, p1)
    resid_ref[...] = rhs - step1 * image1 - step2 * image2
    for j in range(own_cols):
        dens_ref[:, j * patch : (j + 1) * patch] = (
            step1 * g1_wide[j * d : (j + 1) * d] + step2 * g2_wide[j * d : (j + 1) * d]
        )
    sum_ref[...] = jnp.zeros((2 * d, patch), f32)

    @pl.when(odd == 0)
    def _():
        for s in range(2):
            remote(ev_out, ev_in.at[s], ev_ss, ev_rs.at[s], my_r, my_c).wait_recv()
        sum_ref[...] = ev_in[0].astype(f32) + ev_in[1].astype(f32)

    fc.wait_recv()
    field = sum_ref[...]
    for c in range(nc):
        field = field + fc_in[c].astype(f32)
    far = step1 * field[:d] + step2 * field[d:]
    for row in range(d):
        far_ref[:, row * patch : (row + 1) * patch] = far[row : row + 1]
    ev.wait_send()
    p1.wait_send()
    fc.wait_send()


def hand_on(*refs):
    count = len(refs) // 2
    sems = refs[-1]
    copies = [
        pltpu.make_async_copy(refs[n], refs[count + n], sems.at[n]) for n in range(count)
    ]
    for copy in copies:
        copy.start()
    for copy in copies:
        copy.wait()


def per_device(nr, nc, right_side, u_factors, v_factors, ranks, far_blocks, block_target, recv_order):
    dens_count, patch = right_side.shape
    own_rows, all_cols, slot_count, _ = u_factors.shape
    group_rows, own_cols = v_factors.shape[:2]
    block_count, _, unknowns = far_blocks.shape
    recv_total = recv_order.shape[0]
    assert own_rows == 1 and group_rows == nc and all_cols == nc * own_cols
    assert block_count == 2 and recv_total == nr * nc and unknowns == own_cols * patch
    slots = own_cols * slot_count
    rows = own_cols * dens_count
    chunk = rows // nr
    half = -(-slots // (2 * LANES)) * LANES
    bf = jnp.bfloat16
    f32 = jnp.float32
    wire = bf if chunk % 16 == 0 else f32
    dma = pltpu.SemaphoreType.DMA
    u = u_factors.reshape(nc, slots, patch)
    v = v_factors.reshape(group_rows, slots, patch)
    vmem = pl.BlockSpec(memory_space=pltpu.VMEM)
    smem = pl.BlockSpec(memory_space=pltpu.SMEM)
    hbm = pl.BlockSpec(memory_space=pl.ANY)
    scratch = [
        pltpu.VMEM(u.shape, bf),
        pltpu.VMEM(v.shape, bf),
        pltpu.VMEM(far_blocks.shape, bf),
        pltpu.VMEM((nc, slots), f32),
        pltpu.VMEM((nr, chunk, patch), f32),
        pltpu.VMEM((2 * dens_count, patch), f32),
        pltpu.VMEM((4, nc, 2 * dens_count, half), bf),
        pltpu.VMEM((4, nc, 2 * dens_count, half), bf),
        pltpu.VMEM((2, nr, chunk, patch), wire),
        pltpu.VMEM((2, nr, chunk, patch), wire),
        pltpu.VMEM((2, nr, chunk, patch), wire),
        pltpu.VMEM((2, nc, dens_count, LANES), f32),
        pltpu.VMEM((2, nr, dens_count, LANES), f32),
        pltpu.VMEM((nr, 2 * dens_count, patch), bf),
        pltpu.VMEM((nc, 2 * dens_count, patch), bf),
        pltpu.VMEM((nc, 2 * dens_count, patch), bf),
        pltpu.VMEM((2 * dens_count, patch), bf),
        pltpu.VMEM((2, 2 * dens_count, patch), bf),
        dma((4,)),
        dma((4,)), dma((4,)),
        dma((2,)), dma((2,)),
        dma((2,)), dma((2,)),
        dma((2,)), dma((2,)),
        dma((2,)), dma((2,)),
        dma, dma,
        dma, dma,
        dma, dma((2,)),
    ]
    matrix = u.size + v.size
    results = pl.pallas_call(
        functools.partial(kernel, nr, nc, dens_count, own_cols, slot_count, patch),
        out_shape=(
            jax.ShapeDtypeStruct((dens_count, unknowns), f32),
            jax.ShapeDtypeStruct((dens_count, patch), f32),
            jax.ShapeDtypeStruct((1, dens_count * patch), f32),
        ),
        in_specs=[vmem, vmem, smem, smem, hbm, hbm, hbm],
        out_specs=(vmem, vmem, vmem),
        scratch_shapes=scratch,
        compiler_params=pltpu.CompilerParams(
            collective_id=0, has_side_effects=True, vmem_limit_bytes=56 * 1024 * 1024
        ),
        cost_estimate=pl.CostEstimate(
            flops=8 * dens_count * matrix + 2 * dens_count * far_blocks.size,
            bytes_accessed=2 * (matrix + far_blocks.size), transcendentals=0,
        ),
    )(right_side, ranks, block_target, recv_order, u, v, far_blocks)
    return pl.pallas_call(
        hand_on,
        out_shape=tuple(jax.ShapeDtypeStruct(x.shape, x.dtype) for x in results),
        in_specs=[pl.BlockSpec(memory_space=pltpu.HBM)] * len(results),
        out_specs=(pl.BlockSpec(memory_space=pltpu.HBM),) * len(results),
        scratch_shapes=[dma((len(results),))],
    )(*results)


def solution(mesh):
    return jax.shard_map(
        functools.partial(per_device, mesh.shape["row"], mesh.shape["col"]),
        mesh=mesh,
        in_specs=(
            P(None, ("row", "col")),
            P(("row", "col"), None, None, None),
            P("row", "col", None, None),
            P("row", "col"),
            P("row", None, "col"),
            P(),
            P(),
        ),
        out_specs=(P(None, "col"), P(None, ("row", "col")), P(("row", "col"), None)),
        check_vma=False,
    )
```

time: 57.6 us -> 55.8 us (0.969)
  local copies, waits for them, and re-layouts: 4.21 us -> 0 us
  Pallas kernels: 52.3 us -> 55 us
    pallas_call x0 -> x1, Pallas kernels: none -> 6.09 us  [per_device(): pl.pallas_call(hand_on, out_shape=tuple((jax.ShapeDtypeStruct(x.shape, x....]
    unnamed x3 -> x0, local copies, waits for them, and re-layouts: 4.21 us -> none
    pallas_call x1, Pallas kernels: 52.3 us -> 48.9 us  [per_device(): pl.pallas_call(functools.partial(kernel, nr, nc, dens_count, own_cols, sl...]
where the time goes in v2:
time: 55.8 us; the launch traced here: 55.6 us
  Pallas kernels  55 us (99%)
  between operations  0.64 us (1%)
    pallas_call x1, Pallas kernels, per_device(): pl.pallas_call(functools.partial(kernel, nr, nc, dens_count, own_cols, sl...  48.9 us
    pallas_call x1, Pallas kernels, per_device(): pl.pallas_call(hand_on, out_shape=tuple((jax.ShapeDtypeStruct(x.shape, x....  6.09 us

profile of v2, /device:TPU:0, one launch (start us, length us, event | category | flops | bytes accessed | tf_op | source)
XLA Modules:
  0.0 55.6 jit_solution(6377122893097542284)
XLA Ops:
  0.6 48.9 %shard_map.94 = (f32[8,4096]{1,0:T(8,128)}, f32[8,512]{1,0:T(8,128)}, f32[1,4096]{1,0:T(1,128)}) custom-call(f32[8,512]{1,0:T(8,128)} %rhs_ref.1, s32[8,8]{1,0:T(8,128)} %ranks_ref.1, s32[8,8]{1,0:T(8,128)} %target_ref.1, s32[32]{0:T(128)} %order_ref.1, bf16[8,384,512]{2,1,0:T(8,128)(2,1)} %bitcast.2, bf16[8,384,512]{2,1,0:T(8,128)(2,1)} %bitcast.3, ...), custom_call_target="tpu_custom_call" | custom-call | flops 268435456 | bytes 14680064 | tf_op jit(solution)/shard_map/pallas_call | solution.py:359
  49.5 6.1 %shard_map.95 = (f32[8,4096]{1,0:T(8,128)}, f32[8,512]{1,0:T(8,128)}, f32[1,4096]{1,0:T(1,128)}) custom-call(f32[8,4096]{1,0:T(8,128)} %get-tuple-element.6.refs_0_, f32[8,512]{1,0:T(8,128)} %get-tuple-element.7.refs_1_, f32[1,4096]{1,0:T(1,128)} %get-tuple-element.8.refs_2_), custom_call_target="tpu_custom_call" | custom-call | tf_op jit(solution)/shard_map/pallas_call | solution.py:377

commit v3 on v2

--- a/solution.py
+++ b/solution.py
@@ -26,10 +26,10 @@
 
 
 def kernel(
-    nr, nc, dens_count, own_cols, slot_count, patch,
+    nr, nc, dens_count, own_cols, slot_count, patch, pair,
     rhs_ref, ranks_ref, target_ref, order_ref, u_hbm, v_hbm, f_hbm,
     dens_ref, resid_ref, far_ref,
-    u_v, v_v, f_v, kept_ref, acc_ref, sum_ref,
+    u_v, v_v, f_v, x_v, kept_ref, acc_ref, sum_ref,
     a2a_out, a2a_in, rs_out, rs_in, ag_buf, sc_col, sc_row, z_buf, fc_out, fc_in, ev_out, ev_in,
     load_sem, a2a_ss, a2a_rs, rs_ss, rs_rs, ag_ss, ag_rs,
     scc_ss, scc_rs, scr_ss, scr_rs, z_ss, z_rs, fc_ss, fc_rs, ev_ss, ev_rs,
@@ -85,28 +85,43 @@
         x = x.astype(f32)
         return jnp.concatenate([x[:d], x[d:, : slots - half]], axis=1)
 
-    def exchange(rnd, values):
-        for c in range(nc):
-            a2a_out[rnd, c] = pack(values[c])
+    wide = pair * slots
+    lane_col = lax.broadcasted_iota(jnp.int32, (d, wide), 1) % slots // slot_count
+    diag = jnp.concatenate([(lane_col == j).astype(f32) for j in range(own_cols)], axis=0)
+
+    def group(ref, q):
+        return ref[pl.ds(pl.multiple_of(q * wide, wide), wide), :]
+
+    def put(rnd, q, value):
+        for n in range(pair):
+            a2a_out[rnd, q * pair + n] = pack(value[:, n * slots : (n + 1) * slots])
+
+    def got(rnd, q):
+        return jnp.concatenate([unpack(a2a_in[rnd, q * pair + n]) for n in range(pair)], axis=1)
+
+    def exchange(rnd):
         sent = over_col(a2a_out.at[rnd], a2a_in.at[rnd], a2a_ss.at[rnd], a2a_rs.at[rnd])
         a2a_in[rnd, my_c] = a2a_out[rnd, my_c]
         return sent
 
-    lane_col = lax.broadcasted_iota(jnp.int32, (d, slots), 1) // slot_count
-    diag = jnp.concatenate([(lane_col == j).astype(f32) for j in range(own_cols)], axis=0)
-
-    def back_of(r):
+    def back_of(rnd, r):
         rb = r.astype(bf)
-        return [
-            lax.dot_general(rb, u_v[c], NT, preferred_element_type=f32) for c in range(nc)
-        ]
+
+        def body(q, _):
+            put(rnd, q, lax.dot_general(rb, group(u_v, q), NT, preferred_element_type=f32))
+            return _
+
+        lax.fori_loop(0, nc // pair, body, 0, unroll=2)
 
     def grad_of(rnd):
-        acc = jnp.zeros((rows, patch), f32)
-        for c in range(nc):
-            b = unpack(a2a_in[rnd, c]) * kept_ref[c : c + 1, :]
-            wide = (jnp.concatenate([b] * own_cols, axis=0) * diag).astype(bf)
-            acc = acc + lax.dot_general(wide, v_v[c], NN, preferred_element_type=f32)
+        def body(q, acc):
+            b = got(rnd, q) * kept_ref[pl.ds(q, 1), :]
+            spread = (jnp.concatenate([b] * own_cols, axis=0) * diag).astype(bf)
+            return acc + lax.dot_general(spread, group(v_v, q), NN, preferred_element_type=f32)
+
+        acc = lax.fori_loop(
+            0, nc // pair, body, jnp.zeros((rows, patch), f32), unroll=2
+        )
         return acc.reshape(nr, chunk, patch)
 
     def reduce_start(it, acc):
@@ -130,22 +145,23 @@
     def gathered(it):
         return ag_buf[it].reshape(rows, patch).astype(bf)
 
-    def coef_of(g):
-        values = []
-        for c in range(nc):
-            wide = lax.dot_general(g, v_v[c], NT, preferred_element_type=f32) * diag
-            part = wide[:d]
+    def coef_of(rnd, g):
+        def body(q, _):
+            full = lax.dot_general(g, group(v_v, q), NT, preferred_element_type=f32) * diag
+            part = full[:d]
             for j in range(1, own_cols):
-                part = part + wide[j * d : (j + 1) * d]
-            values.append(part * kept_ref[c : c + 1, :])
-        return values
+                part = part + full[j * d : (j + 1) * d]
+            put(rnd, q, part * kept_ref[pl.ds(q, 1), :])
+            return _
+
+        lax.fori_loop(0, nc // pair, body, 0, unroll=2)
 
     def image_of(rnd):
-        image = jnp.zeros((d, patch), f32)
-        for c in range(nc):
-            coef = unpack(a2a_in[rnd, c]).astype(bf)
-            image = image + lax.dot_general(coef, u_v[c], NN, preferred_element_type=f32)
-        return image
+        def body(q, image):
+            coef = got(rnd, q).astype(bf)
+            return image + lax.dot_general(coef, group(u_v, q), NN, preferred_element_type=f32)
+
+        return lax.fori_loop(0, nc // pair, body, jnp.zeros((d, patch), f32), unroll=2)
 
     lane = lax.broadcasted_iota(jnp.int32, (d, LANES), 1)
 
@@ -183,12 +199,14 @@
     limit = jnp.zeros((nc, slots), jnp.int32)
     for j in range(own_cols):
         limit = jnp.where(lane_all // slot_count == j, ranks[:, j : j + 1], limit)
-    kept_ref[...] = (lane_all % slot_count < limit).astype(f32)
+    kept = (lane_all % slot_count < limit).astype(f32)
+    for c in range(nc):
+        kept_ref[c // pair : c // pair + 1, pl.ds(c % pair * slots, slots)] = kept[c : c + 1]
     u_copy.wait()
     v_copy.start()
-    back0 = back_of(rhs)
+    back_of(0, rhs)
     pl.semaphore_wait(barrier, nc - 1 + nr - 1)
-    x0 = exchange(0, back0)
+    x0 = exchange(0)
     v_copy.wait()
     for copy in f_copies[::-1]:
         copy.start()
@@ -200,11 +218,13 @@
     s0.wait_send()
     a0.wait_recv()
     g1_all = gathered(0)
-    x1 = exchange(1, coef_of(g1_all))
+    coef_of(1, g1_all)
+    x1 = exchange(1)
     a0.wait_send()
     x1.wait_recv()
     image1 = image_of(1)
-    x2 = exchange(2, back_of(image1))
+    back_of(2, image1)
+    x2 = exchange(2)
     q0 = squares_out(0, g1, image1)
     x1.wait_send()
     x2.wait_recv()
@@ -221,21 +241,26 @@
     p0.wait_send()
     a1.wait_recv()
     g2_all = gathered(1)
-    x3 = exchange(3, coef_of(g2_all))
+    coef_of(3, g2_all)
+    x3 = exchange(3)
 
     g1_wide = g1_all.astype(f32)
     g2_wide = g2_all.astype(f32)
 
+    for j in range(own_cols):
+        x_v[:, j * patch : (j + 1) * patch] = jnp.concatenate(
+            [g1_wide[j * d : (j + 1) * d], g2_wide[j * d : (j + 1) * d]], axis=0
+        ).astype(bf)
+
     def field_of(b):
-        field = jnp.zeros((2 * d, patch), f32)
-        for j in range(own_cols):
-            lhs = jnp.concatenate(
-                [g1_wide[j * d : (j + 1) * d], g2_wide[j * d : (j + 1) * d]], axis=0
-            ).astype(bf)
-            field = field + lax.dot_general(
-                lhs, f_v[b, :, j * patch : (j + 1) * patch], NT, preferred_element_type=f32
+        def body(j, field):
+            at = pl.ds(pl.multiple_of(j * patch, patch), patch)
+            return field + lax.dot_general(
+                x_v[:, at], f_v[b, :, at], NT, preferred_element_type=f32
             )
-        return field.astype(bf)
+
+        start = jnp.zeros((2 * d, patch), f32)
+        return lax.fori_loop(0, own_cols, body, start, unroll=2).astype(bf)
 
     for copy in f_copies:
         copy.wait()
@@ -295,14 +320,8 @@
 
 def hand_on(*refs):
     count = len(refs) // 2
-    sems = refs[-1]
-    copies = [
-        pltpu.make_async_copy(refs[n], refs[count + n], sems.at[n]) for n in range(count)
-    ]
-    for copy in copies:
-        copy.start()
-    for copy in copies:
-        copy.wait()
+    for n in range(count):
+        refs[count + n][...] = refs[n][...]
 
 
 def per_device(nr, nc, right_side, u_factors, v_factors, ranks, far_blocks, block_target, recv_order):
@@ -321,8 +340,9 @@
     f32 = jnp.float32
     wire = bf if chunk % 16 == 0 else f32
     dma = pltpu.SemaphoreType.DMA
-    u = u_factors.reshape(nc, slots, patch)
-    v = v_factors.reshape(group_rows, slots, patch)
+    pair = 2 if nc % 2 == 0 else 1
+    u = u_factors.reshape(nc * slots, patch)
+    v = v_factors.reshape(nc * slots, patch)
     vmem = pl.BlockSpec(memory_space=pltpu.VMEM)
     smem = pl.BlockSpec(memory_space=pltpu.SMEM)
     hbm = pl.BlockSpec(memory_space=pl.ANY)
@@ -330,7 +350,8 @@
         pltpu.VMEM(u.shape, bf),
         pltpu.VMEM(v.shape, bf),
         pltpu.VMEM(far_blocks.shape, bf),
-        pltpu.VMEM((nc, slots), f32),
+        pltpu.VMEM((2 * dens_count, unknowns), bf),
+        pltpu.VMEM((nc // pair, pair * slots), f32),
         pltpu.VMEM((nr, chunk, patch), f32),
         pltpu.VMEM((2 * dens_count, patch), f32),
         pltpu.VMEM((4, nc, 2 * dens_count, half), bf),
@@ -357,7 +378,7 @@
     ]
     matrix = u.size + v.size
     results = pl.pallas_call(
-        functools.partial(kernel, nr, nc, dens_count, own_cols, slot_count, patch),
+        functools.partial(kernel, nr, nc, dens_count, own_cols, slot_count, patch, pair),
         out_shape=(
             jax.ShapeDtypeStruct((dens_count, unknowns), f32),
             jax.ShapeDtypeStruct((dens_count, patch), f32),
@@ -377,9 +398,8 @@
     return pl.pallas_call(
         hand_on,
         out_shape=tuple(jax.ShapeDtypeStruct(x.shape, x.dtype) for x in results),
-        in_specs=[pl.BlockSpec(memory_space=pltpu.HBM)] * len(results),
-        out_specs=(pl.BlockSpec(memory_space=pltpu.HBM),) * len(results),
-        scratch_shapes=[dma((len(results),))],
+        in_specs=[vmem] * len(results),
+        out_specs=(vmem,) * len(results),
     )(*results)
 
 

time: 55.8 us -> 52.4 us (0.939)
  Pallas kernels: 55 us -> 51.5 us
    pallas_call x1, Pallas kernels: 6.09 us -> 1.59 us  [per_device(): pl.pallas_call(hand_on, out_shape=tuple((jax.ShapeDtypeStruct(x.shape, x....]
    pallas_call x1, Pallas kernels: 48.9 us -> 49.9 us  [per_device(): pl.pallas_call(functools.partial(kernel, nr, nc, dens_count, own_cols, sl...]
where the time goes in v3:
time: 52.4 us; the launch traced here: 52.1 us
  Pallas kernels  51.5 us (98%)
  between operations  0.64 us (1%)
    pallas_call x1, Pallas kernels, per_device(): pl.pallas_call(functools.partial(kernel, nr, nc, dens_count, own_cols, sl...  49.9 us
    pallas_call x1, Pallas kernels, per_device(): pl.pallas_call(hand_on, out_shape=tuple((jax.ShapeDtypeStruct(x.shape, x....  1.59 us

profile of v3, /device:TPU:0, one launch (start us, length us, event | category | flops | bytes accessed | tf_op | source)
XLA Modules:
  0.0 52.1 jit_solution(12195629161887944431)
XLA Ops:
  0.6 49.9 %shard_map.94 = (f32[8,4096]{1,0:T(8,128)}, f32[8,512]{1,0:T(8,128)}, f32[1,4096]{1,0:T(1,128)}) custom-call(f32[8,512]{1,0:T(8,128)} %rhs_ref.1, s32[8,8]{1,0:T(8,128)} %ranks_ref.1, s32[8,8]{1,0:T(8,128)} %target_ref.1, s32[32]{0:T(128)} %order_ref.1, bf16[3072,512]{1,0:T(8,128)(2,1)} %bitcast.2, bf16[3072,512]{1,0:T(8,128)(2,1)} %bitcast.3, ...), custom_call_target="tpu_custom_call" | custom-call | flops 268435456 | bytes 14680064 | tf_op jit(solution)/shard_map/pallas_call | solution.py:380
  50.5 1.6 %shard_map.95 = (f32[8,4096]{1,0:T(8,128)}, f32[8,512]{1,0:T(8,128)}, f32[1,4096]{1,0:T(1,128)}) custom-call(f32[8,4096]{1,0:T(8,128)} %get-tuple-element.6.refs_0_, f32[8,512]{1,0:T(8,128)} %get-tuple-element.7.refs_1_, f32[1,4096]{1,0:T(1,128)} %get-tuple-element.8.refs_2_), custom_call_target="tpu_custom_call" | custom-call | tf_op jit(solution)/shard_map/pallas_call | solution.py:398

commit v4 on v3

v4 whole, which is shorter than its diff:
```python
import functools

import jax
import jax.numpy as jnp
from jax import lax
from jax.experimental import pallas as pl
from jax.experimental.pallas import tpu as pltpu
from jax.sharding import PartitionSpec as P

MESH = pl.DeviceIdType.MESH
LANES = 128
NT = (((1,), (1,)), ((), ()))
NN = (((1,), (0,)), ((), ()))


def partner_of(me, k, n):
    if n & (n - 1):
        return (me + k) % n
    out = 0
    bit = 1
    while bit < n:
        mine = (me // bit) % 2
        out = out + bit * ((1 - mine) if k & bit else mine)
        bit *= 2
    return out


def kernel(
    nr, nc, dens_count, own_cols, slot_count, patch, pair,
    rhs_hbm, ranks_hbm, target_hbm, order_hbm, u_hbm, v_hbm, f_hbm,
    dens_ref, resid_ref, far_ref,
    rhs_ref, ranks_ref, target_ref, order_ref,
    u_v, v_v, f_v, x_v, kept_ref, acc_ref, sum_ref,
    a2a_out, a2a_in, rs_out, rs_in, ag_buf, sc_col, sc_row, z_buf, fc_out, fc_in, ev_out, ev_in,
    small_sem, u_sem, v_sem, f_sem, a2a_ss, a2a_rs, rs_ss, rs_rs, ag_ss, ag_rs,
    scc_ss, scc_rs, scr_ss, scr_rs, z_ss, z_rs, fc_ss, fc_rs, ev_ss, ev_rs,
):
    d = dens_count
    slots = own_cols * slot_count
    half = a2a_out.shape[-1]
    rows = own_cols * d
    chunk = rows // nr
    groups = nc // pair
    wide = pair * slots
    part = patch // 2
    my_r = lax.axis_index("row")
    my_c = lax.axis_index("col")
    col_peers = [partner_of(my_c, k, nc) for k in range(nc - 1, 0, -1)]
    row_peers = [partner_of(my_r, k, nr) for k in range(nr - 1, 0, -1)]
    bf = jnp.bfloat16
    f32 = jnp.float32

    small = [
        pltpu.make_async_copy(src, dst, small_sem.at[n])
        for n, (src, dst) in enumerate(
            (
                (rhs_hbm, rhs_ref), (ranks_hbm, ranks_ref), (target_hbm, target_ref),
                (order_hbm, order_ref),
            )
        )
    ]
    u_copies, v_copies = [], []
    for q in range(groups):
        at = slice(q * wide, (q + 1) * wide)
        u_copies.append(pltpu.make_async_copy(u_hbm.at[at], u_v.at[at], u_sem.at[q]))
        v_copies.append(pltpu.make_async_copy(v_hbm.at[at], v_v.at[at], v_sem.at[q]))
    f_copies = []
    for b in range(2):
        for h in range(2):
            at = slice(h * part, (h + 1) * part)
            f_copies.append(
                pltpu.make_async_copy(f_hbm.at[b, at], f_v.at[b, at], f_sem.at[2 * b + h])
            )
    for copy in small[:2] + u_copies + small[2:]:
        copy.start()

    barrier = pltpu.get_barrier_semaphore()
    for to in col_peers:
        pl.semaphore_signal(barrier, inc=1, device_id=(my_r, to), device_id_type=MESH)
    for to in row_peers:
        pl.semaphore_signal(barrier, inc=1, device_id=(to, my_c), device_id_type=MESH)

    def remote(src, dst, ssem, rsem, r, c):
        return pltpu.make_async_remote_copy(
            src_ref=src, dst_ref=dst, send_sem=ssem, recv_sem=rsem,
            device_id=(r, c), device_id_type=MESH,
        )

    def over_col(out, into, ssem, rsem, shared=False):
        for to in col_peers:
            src = out.at[my_c] if shared else out.at[to]
            remote(src, into.at[my_c], ssem, rsem, my_r, to).start()
        return remote(out.at[: nc - 1], into.at[: nc - 1], ssem, rsem, my_r, my_c)

    def over_row(out, into, ssem, rsem, shared=False):
        for to in row_peers:
            src = out.at[my_r] if shared else out.at[to]
            remote(src, into.at[my_r], ssem, rsem, to, my_c).start()
        return remote(out.at[: nr - 1], into.at[: nr - 1], ssem, rsem, my_r, my_c)

    def pack(x):
        top, low = x[:, :half], x[:, half:]
        if low.shape[1] < half:
            low = jnp.concatenate([low, jnp.zeros((d, half - low.shape[1]), f32)], axis=1)
        return jnp.concatenate([top, low], axis=0).astype(bf)

    def unpack(x):
        x = x.astype(f32)
        return jnp.concatenate([x[:d], x[d:, : slots - half]], axis=1)

    lane_col = lax.broadcasted_iota(jnp.int32, (d, wide), 1) % slots // slot_count
    diag = jnp.concatenate([(lane_col == j).astype(f32) for j in range(own_cols)], axis=0)

    def put(rnd, q, value):
        for n in range(pair):
            a2a_out[rnd, q * pair + n] = pack(value[:, n * slots : (n + 1) * slots])

    def got(rnd, q):
        return jnp.concatenate([unpack(a2a_in[rnd, q * pair + n]) for n in range(pair)], axis=1)

    def exchange(rnd):
        sent = over_col(a2a_out.at[rnd], a2a_in.at[rnd], a2a_ss.at[rnd], a2a_rs.at[rnd])
        a2a_in[rnd, my_c] = a2a_out[rnd, my_c]
        return sent

    def back_of(rnd, r, first):
        rb = r.astype(bf)
        for q in range(groups):
            if first:
                u_copies[q].wait()
                v_copies[q].start()
            u = u_v[q * wide : (q + 1) * wide, :]
            put(rnd, q, lax.dot_general(rb, u, NT, preferred_element_type=f32))

    def image_of(rnd):
        image = jnp.zeros((d, patch), f32)
        for q in range(groups):
            u = u_v[q * wide : (q + 1) * wide, :]
            image = image + lax.dot_general(
                got(rnd, q).astype(bf), u, NN, preferred_element_type=f32
            )
        return image

    def grad_start(it, rnd):
        spread = []
        for q in range(groups):
            b = got(rnd, q) * kept_ref[q : q + 1, :]
            spread.append((jnp.concatenate([b] * own_cols, axis=0) * diag).astype(bf))
        sent = []
        for h in range(2):
            acc = jnp.zeros((rows, part), f32)
            for q in range(groups):
                v = v_v[q * wide : (q + 1) * wide, h * part : (h + 1) * part]
                acc = acc + lax.dot_general(spread[q], v, NN, preferred_element_type=f32)
            acc = acc.reshape(nr, chunk, part)
            rs_out[it, h] = acc.astype(rs_out.dtype)
            sent.append(
                over_row(rs_out.at[it, h], rs_in.at[it, h], rs_ss.at[it, h], rs_rs.at[it, h])
            )
            acc_ref[h] = acc
            rs_in[it, h, my_r] = jnp.zeros((chunk, part), rs_in.dtype)
        return sent

    def grad_end(it, h, sent):
        total = acc_ref[h, my_r]
        sent[h].wait_recv()
        for r in range(nr):
            total = total + rs_in[it, h, r].astype(f32)
        return total

    def gather_start(it, h, g):
        ag_buf[it, h, my_r] = g.astype(ag_buf.dtype)
        return over_row(
            ag_buf.at[it, h], ag_buf.at[it, h], ag_ss.at[it, h], ag_rs.at[it, h], shared=True
        )

    def gathered(it, h):
        return ag_buf[it, h].reshape(rows, part)

    def coef_of(rnd, it, sent):
        parts = [jnp.zeros((d, wide), f32)] * groups
        for h in range(2):
            sent[h].wait_recv()
            g = gathered(it, h).astype(bf)
            for q in range(groups):
                v = v_v[q * wide : (q + 1) * wide, h * part : (h + 1) * part]
                full = lax.dot_general(g, v, NT, preferred_element_type=f32) * diag
                for j in range(own_cols):
                    parts[q] = parts[q] + full[j * d : (j + 1) * d]
        for q in range(groups):
            put(rnd, q, parts[q] * kept_ref[q : q + 1, :])

    lane = lax.broadcasted_iota(jnp.int32, (d, LANES), 1)

    def squares_out(it, halves, image):
        squares = jnp.zeros((d, part), f32)
        for g in halves:
            for j in range(chunk // d):
                squares = squares + g[j * d : (j + 1) * d] * g[j * d : (j + 1) * d]
        grad_sq = jnp.sum(squares, axis=1, keepdims=True)
        image_sq = jnp.sum(image * image, axis=1, keepdims=True)
        sc_col[it, my_c] = jnp.where(lane < LANES // 2, grad_sq, image_sq)
        return over_col(
            sc_col.at[it], sc_col.at[it], scc_ss.at[it], scc_rs.at[it], shared=True
        )

    def squares_on(it, sent):
        sent.wait_recv()
        total = sc_col[it, 0]
        for c in range(1, nc):
            total = total + sc_col[it, c]
        sc_row[it, my_r] = total
        return over_row(
            sc_row.at[it], sc_row.at[it], scr_ss.at[it], scr_rs.at[it], shared=True
        )

    def squares_in(it, sent):
        sent.wait_recv()
        total = sc_row[it, 0]
        for r in range(1, nr):
            total = total + sc_row[it, r]
        return total[:, :1] / (total[:, LANES // 2 : LANES // 2 + 1] + 1e-6)

    small[1].wait()
    lane_all = lax.broadcasted_iota(jnp.int32, (nc, slots), 1)
    ranks = ranks_ref[...]
    limit = jnp.zeros((nc, slots), jnp.int32)
    for j in range(own_cols):
        limit = jnp.where(lane_all // slot_count == j, ranks[:, j : j + 1], limit)
    kept = (lane_all % slot_count < limit).astype(f32)
    for c in range(nc):
        at = pl.ds(c % pair * slots, slots)
        kept_ref[c // pair : c // pair + 1, at] = kept[c : c + 1]
    small[0].wait()
    rhs = rhs_ref[...]
    back_of(0, rhs, True)
    pl.semaphore_wait(barrier, nc - 1 + nr - 1)
    x0 = exchange(0)
    for copy in v_copies:
        copy.wait()
    for copy in f_copies[2:] + f_copies[:2]:
        copy.start()
    x0.wait_recv()
    s0 = grad_start(0, 0)
    x0.wait_send()
    g1, a0 = [], []
    for h in range(2):
        g1.append(grad_end(0, h, s0))
        a0.append(gather_start(0, h, g1[h]))
    for sent in s0:
        sent.wait_send()
    coef_of(1, 0, a0)
    x1 = exchange(1)
    for sent in a0:
        sent.wait_send()
    x1.wait_recv()
    image1 = image_of(1)
    back_of(2, image1, False)
    x2 = exchange(2)
    q0 = squares_out(0, g1, image1)
    x1.wait_send()
    x2.wait_recv()
    s1 = grad_start(1, 2)
    p0 = squares_on(0, q0)

    step1 = squares_in(0, p0)
    step_rows = jnp.concatenate([step1] * (chunk // d), axis=0)
    g2, a1 = [], []
    for h in range(2):
        g2.append(g1[h] - step_rows * grad_end(1, h, s1))
        a1.append(gather_start(1, h, g2[h]))
    x2.wait_send()
    for sent in s1:
        sent.wait_send()
    q0.wait_send()
    p0.wait_send()
    coef_of(3, 1, a1)
    x3 = exchange(3)

    for h in range(2):
        one, two = gathered(0, h).astype(f32), gathered(1, h).astype(f32)
        for j in range(own_cols):
            x_v[:, j * patch + h * part : j * patch + (h + 1) * part] = jnp.concatenate(
                [one[j * d : (j + 1) * d], two[j * d : (j + 1) * d]], axis=0
            ).astype(bf)

    def field_of(b):
        field = jnp.zeros((2 * d, patch), f32)
        for j in range(own_cols):
            at = slice(j * patch, (j + 1) * patch)
            field = field + lax.dot_general(
                x_v[:, at], f_v[b, :, at], NT, preferred_element_type=f32
            )
        return field.astype(bf)

    for copy in f_copies + small[2:]:
        copy.wait()
    z_buf[my_r] = field_of(1)
    z = over_row(z_buf, z_buf, z_ss, z_rs, shared=True)
    x3.wait_recv()
    image2 = image_of(3)
    q1 = squares_out(1, g2, image2)

    z.wait_recv()
    fields = [z_buf[r].astype(f32) for r in range(nr)]
    targets = [target_ref[2 * r + 1, my_c] for r in range(nr)]
    for to in range(nc):
        wanted = order_ref[my_r * nc + to]
        mixed = jnp.zeros((2 * d, patch), f32)
        for r in range(nr):
            mixed = mixed + fields[r] * jnp.where(targets[r] == wanted, 1.0, 0.0).astype(f32)
        fc_out[to] = mixed.astype(bf)
    fc = over_col(fc_out, fc_in, fc_ss, fc_rs)
    fc_in[my_c] = fc_out[my_c]

    ev_out[...] = field_of(0)
    odd = my_c % 2
    ev_row = (1 - odd) * ((my_r + nr // 2) % nr) + odd * my_r
    ev = remote(ev_out, ev_in.at[odd], ev_ss, ev_rs.at[odd], ev_row, my_c - odd)
    ev.start()
    p1 = squares_on(1, q1)
    x3.wait_send()
    for sent in a1:
        sent.wait_send()
    z.wait_send()
    q1.wait_send()
    fc.wait_recv()
    field = fc_in[0].astype(f32)
    for c in range(1, nc):
        field = field + fc_in[c].astype(f32)
    sum_ref[...] = field
    step2 = squares_in(1, p1)
    resid_ref[...] = rhs - step1 * image1 - step2 * image2
    for h in range(2):
        one, two = gathered(0, h).astype(f32), gathered(1, h).astype(f32)
        for j in range(own_cols):
            dens_ref[:, j * patch + h * part : j * patch + (h + 1) * part] = (
                step1 * one[j * d : (j + 1) * d] + step2 * two[j * d : (j + 1) * d]
            )

    @pl.when(odd == 0)
    def _():
        for s in range(2):
            remote(ev_out, ev_in.at[s], ev_ss, ev_rs.at[s], my_r, my_c).wait_recv()
        sum_ref[...] += ev_in[0].astype(f32) + ev_in[1].astype(f32)

    field = sum_ref[...]
    far = step1 * field[:d] + step2 * field[d:]
    for row in range(d):
        far_ref[:, row * patch : (row + 1) * patch] = far[row : row + 1]
    ev.wait_send()
    p1.wait_send()
    fc.wait_send()


def hand_on(*refs):
    count = len(refs) // 2
    for n in range(count):
        refs[count + n][...] = refs[n][...]


def per_device(nr, nc, right_side, u_factors, v_factors, ranks, far_blocks, block_target, recv_order):
    dens_count, patch = right_side.shape
    own_rows, all_cols, slot_count, _ = u_factors.shape
    group_rows, own_cols = v_factors.shape[:2]
    block_count, _, unknowns = far_blocks.shape
    recv_total = recv_order.shape[0]
    assert own_rows == 1 and group_rows == nc and all_cols == nc * own_cols
    assert block_count == 2 and recv_total == nr * nc and unknowns == own_cols * patch
    slots = own_cols * slot_count
    rows = own_cols * dens_count
    chunk = rows // nr
    part = patch // 2
    half = -(-slots // (2 * LANES)) * LANES
    bf = jnp.bfloat16
    f32 = jnp.float32
    wire = bf if chunk % 16 == 0 else f32
    dma = pltpu.SemaphoreType.DMA
    pair = 2 if nc % 2 == 0 else 1
    u = u_factors.reshape(nc * slots, patch)
    v = v_factors.reshape(nc * slots, patch)
    vmem = pl.BlockSpec(memory_space=pltpu.VMEM)
    hbm = pl.BlockSpec(memory_space=pl.ANY)
    scratch = [
        pltpu.VMEM(right_side.shape, f32),
        pltpu.VMEM(ranks.shape, jnp.int32),
        pltpu.SMEM(block_target.shape, jnp.int32),
        pltpu.SMEM(recv_order.shape, jnp.int32),
        pltpu.VMEM(u.shape, bf),
        pltpu.VMEM(v.shape, bf),
        pltpu.VMEM(far_blocks.shape, bf),
        pltpu.VMEM((2 * dens_count, unknowns), bf),
        pltpu.VMEM((nc // pair, pair * slots), f32),
        pltpu.VMEM((2, nr, chunk, part), f32),
        pltpu.VMEM((2 * dens_count, patch), f32),
        pltpu.VMEM((4, nc, 2 * dens_count, half), bf),
        pltpu.VMEM((4, nc, 2 * dens_count, half), bf),
        pltpu.VMEM((2, 2, nr, chunk, part), wire),
        pltpu.VMEM((2, 2, nr, chunk, part), wire),
        pltpu.VMEM((2, 2, nr, chunk, part), wire),
        pltpu.VMEM((2, nc, dens_count, LANES), f32),
        pltpu.VMEM((2, nr, dens_count, LANES), f32),
        pltpu.VMEM((nr, 2 * dens_count, patch), bf),
        pltpu.VMEM((nc, 2 * dens_count, patch), bf),
        pltpu.VMEM((nc, 2 * dens_count, patch), bf),
        pltpu.VMEM((2 * dens_count, patch), bf),
        pltpu.VMEM((2, 2 * dens_count, patch), bf),
        dma((4,)), dma((nc // pair,)), dma((nc // pair,)), dma((4,)),
        dma((4,)), dma((4,)),
        dma((2, 2)), dma((2, 2)),
        dma((2, 2)), dma((2, 2)),
        dma((2,)), dma((2,)),
        dma((2,)), dma((2,)),
        dma, dma,
        dma, dma,
        dma, dma((2,)),
    ]
    matrix = u.size + v.size
    results = pl.pallas_call(
        functools.partial(kernel, nr, nc, dens_count, own_cols, slot_count, patch, pair),
        out_shape=(
            jax.ShapeDtypeStruct((dens_count, unknowns), f32),
            jax.ShapeDtypeStruct((dens_count, patch), f32),
            jax.ShapeDtypeStruct((1, dens_count * patch), f32),
        ),
        in_specs=[hbm] * 7,
        out_specs=(vmem, vmem, vmem),
        scratch_shapes=scratch,
        compiler_params=pltpu.CompilerParams(
            collective_id=0, has_side_effects=True, vmem_limit_bytes=56 * 1024 * 1024
        ),
        cost_estimate=pl.CostEstimate(
            flops=8 * dens_count * matrix + 2 * dens_count * far_blocks.size,
            bytes_accessed=2 * (matrix + far_blocks.size), transcendentals=0,
        ),
    )(right_side, ranks, block_target, recv_order, u, v, far_blocks)
    return pl.pallas_call(
        hand_on,
        out_shape=tuple(jax.ShapeDtypeStruct(x.shape, x.dtype) for x in results),
        in_specs=[vmem] * len(results),
        out_specs=(vmem,) * len(results),
    )(*results)


def solution(mesh):
    return jax.shard_map(
        functools.partial(per_device, mesh.shape["row"], mesh.shape["col"]),
        mesh=mesh,
        in_specs=(
            P(None, ("row", "col")),
            P(("row", "col"), None, None, None),
            P("row", "col", None, None),
            P("row", "col"),
            P("row", None, "col"),
            P(),
            P(),
        ),
        out_specs=(P(None, "col"), P(None, ("row", "col")), P(("row", "col"), None)),
        check_vma=False,
    )
```

time: 52.4 us -> 50.5 us (0.964)
  Pallas kernels: 51.5 us -> 49.7 us
    pallas_call x1, Pallas kernels: 49.9 us -> 48.1 us  [per_device(): pl.pallas_call(functools.partial(kernel, nr, nc, dens_count, own_cols, sl...]
where the time goes in v4:
time: 50.5 us; the launch traced here: 50.4 us
  Pallas kernels  49.7 us (98%)
  between operations  0.64 us (1%)
    pallas_call x1, Pallas kernels, per_device(): pl.pallas_call(functools.partial(kernel, nr, nc, dens_count, own_cols, sl...  48.1 us
    pallas_call x1, Pallas kernels, per_device(): pl.pallas_call(hand_on, out_shape=tuple((jax.ShapeDtypeStruct(x.shape, x....  1.59 us

profile of v4, /device:TPU:0, one launch (start us, length us, event | category | flops | bytes accessed | tf_op | source)
XLA Modules:
  0.0 50.4 jit_solution(2263071477892644496)
XLA Ops:
  0.6 48.1 %shard_map.94 = (f32[8,4096]{1,0:T(8,128)}, f32[8,512]{1,0:T(8,128)}, f32[1,4096]{1,0:T(1,128)}) custom-call(f32[8,512]{1,0:T(8,128)} %rhs_hbm.1, s32[8,8]{1,0:T(8,128)} %ranks_hbm.1, s32[8,8]{1,0:T(8,128)} %target_hbm.1, s32[32]{0:T(128)} %order_hbm.1, bf16[3072,512]{1,0:T(8,128)(2,1)} %bitcast.2, bf16[3072,512]{1,0:T(8,128)(2,1)} %bitcast.3, ...), custom_call_target="tpu_custom_call" | custom-call | flops 268435456 | bytes 14680064 | tf_op jit(solution)/shard_map/pallas_call | solution.py:419
  48.8 1.6 %shard_map.95 = (f32[8,4096]{1,0:T(8,128)}, f32[8,512]{1,0:T(8,128)}, f32[1,4096]{1,0:T(1,128)}) custom-call(f32[8,4096]{1,0:T(8,128)} %get-tuple-element.6.refs_0_, f32[8,512]{1,0:T(8,128)} %get-tuple-element.7.refs_1_, f32[1,4096]{1,0:T(1,128)} %get-tuple-element.8.refs_2_), custom_call_target="tpu_custom_call" | custom-call | tf_op jit(solution)/shard_map/pallas_call | solution.py:437

commit v5 on v4

--- a/solution.py
+++ b/solution.py
@@ -30,17 +30,17 @@
     rhs_hbm, ranks_hbm, target_hbm, order_hbm, u_hbm, v_hbm, f_hbm,
     dens_ref, resid_ref, far_ref,
     rhs_ref, ranks_ref, target_ref, order_ref,
-    u_v, v_v, f_v, x_v, kept_ref, acc_ref, sum_ref,
-    a2a_out, a2a_in, rs_out, rs_in, ag_buf, sc_col, sc_row, z_buf, fc_out, fc_in, ev_out, ev_in,
-    small_sem, u_sem, v_sem, f_sem, a2a_ss, a2a_rs, rs_ss, rs_rs, ag_ss, ag_rs,
+    u_v, v_v, f_v, x_v, kept_ref, g_ref, sum_ref,
+    a2a_out, a2a_in, rd_out, rd_in, sc_col, sc_row, z_buf, fc_out, fc_in, ev_out, ev_in,
+    small_sem, u_sem, v_sem, f_sem, a2a_ss, a2a_rs, rd_ss, rd_rs,
     scc_ss, scc_rs, scr_ss, scr_rs, z_ss, z_rs, fc_ss, fc_rs, ev_ss, ev_rs,
 ):
     d = dens_count
     slots = own_cols * slot_count
     half = a2a_out.shape[-1]
     rows = own_cols * d
-    chunk = rows // nr
     groups = nc // pair
+    stages = rd_out.shape[2]
     wide = pair * slots
     part = patch // 2
     my_r = lax.axis_index("row")
@@ -152,36 +152,39 @@
             for q in range(groups):
                 v = v_v[q * wide : (q + 1) * wide, h * part : (h + 1) * part]
                 acc = acc + lax.dot_general(spread[q], v, NN, preferred_element_type=f32)
-            acc = acc.reshape(nr, chunk, part)
-            rs_out[it, h] = acc.astype(rs_out.dtype)
-            sent.append(
-                over_row(rs_out.at[it, h], rs_in.at[it, h], rs_ss.at[it, h], rs_rs.at[it, h])
-            )
-            acc_ref[h] = acc
-            rs_in[it, h, my_r] = jnp.zeros((chunk, part), rs_in.dtype)
+            sent.append(double(it, h, 0, acc))
         return sent
 
-    def grad_end(it, h, sent):
-        total = acc_ref[h, my_r]
-        sent[h].wait_recv()
-        for r in range(nr):
-            total = total + rs_in[it, h, r].astype(f32)
-        return total
-
-    def gather_start(it, h, g):
-        ag_buf[it, h, my_r] = g.astype(ag_buf.dtype)
-        return over_row(
-            ag_buf.at[it, h], ag_buf.at[it, h], ag_ss.at[it, h], ag_rs.at[it, h], shared=True
+    def double(it, h, stage, value):
+        rd_out[it, h, stage] = value.astype(bf)
+        copy = remote(
+            rd_out.at[it, h, stage], rd_in.at[it, h, stage], rd_ss.at[it, h, stage],
+            rd_rs.at[it, h, stage], partner_of(my_r, 1 << stage, nr), my_c,
         )
-
-    def gathered(it, h):
-        return ag_buf[it, h].reshape(rows, part)
-
-    def coef_of(rnd, it, sent):
+        copy.start()
+        return copy
+
+    def doubled(it, h, stage, copy):
+        copy.wait_recv()
+        return rd_out[it, h, stage].astype(f32) + rd_in[it, h, stage].astype(f32)
+
+    def grad_on(it, sent):
+        flying, done = list(sent), list(sent)
+        for stage in range(stages - 1):
+            for h in range(2):
+                value = doubled(it, h, stage, flying[h])
+                flying[h] = double(it, h, stage + 1, value)
+                done.append(flying[h])
+        return flying, done
+
+    def coef_of(rnd, it, flying, step):
         parts = [jnp.zeros((d, wide), f32)] * groups
         for h in range(2):
-            sent[h].wait_recv()
-            g = gathered(it, h).astype(bf)
+            g = doubled(it, h, stages - 1, flying[h])
+            if step is not None:
+                g = g_ref[0, h] - jnp.concatenate([step] * own_cols, axis=0) * g
+            g_ref[it, h] = g
+            g = g.astype(bf)
             for q in range(groups):
                 v = v_v[q * wide : (q + 1) * wide, h * part : (h + 1) * part]
                 full = lax.dot_general(g, v, NT, preferred_element_type=f32) * diag
@@ -192,12 +195,13 @@
 
     lane = lax.broadcasted_iota(jnp.int32, (d, LANES), 1)
 
-    def squares_out(it, halves, image):
+    def squares_out(it, image):
         squares = jnp.zeros((d, part), f32)
-        for g in halves:
-            for j in range(chunk // d):
-                squares = squares + g[j * d : (j + 1) * d] * g[j * d : (j + 1) * d]
-        grad_sq = jnp.sum(squares, axis=1, keepdims=True)
+        for h in range(2):
+            for j in range(own_cols):
+                g = g_ref[it, h, j * d : (j + 1) * d]
+                squares = squares + g * g
+        grad_sq = jnp.sum(squares, axis=1, keepdims=True) * (1.0 / nr)
         image_sq = jnp.sum(image * image, axis=1, keepdims=True)
         sc_col[it, my_c] = jnp.where(lane < LANES // 2, grad_sq, image_sq)
         return over_col(
@@ -243,42 +247,30 @@
     x0.wait_recv()
     s0 = grad_start(0, 0)
     x0.wait_send()
-    g1, a0 = [], []
-    for h in range(2):
-        g1.append(grad_end(0, h, s0))
-        a0.append(gather_start(0, h, g1[h]))
+    flying, s0 = grad_on(0, s0)
+    coef_of(1, 0, flying, None)
+    x1 = exchange(1)
     for sent in s0:
-        sent.wait_send()
-    coef_of(1, 0, a0)
-    x1 = exchange(1)
-    for sent in a0:
         sent.wait_send()
     x1.wait_recv()
     image1 = image_of(1)
     back_of(2, image1, False)
     x2 = exchange(2)
-    q0 = squares_out(0, g1, image1)
+    q0 = squares_out(0, image1)
     x1.wait_send()
     x2.wait_recv()
     s1 = grad_start(1, 2)
     p0 = squares_on(0, q0)
 
+    flying, s1 = grad_on(1, s1)
+    x2.wait_send()
+    q0.wait_send()
     step1 = squares_in(0, p0)
-    step_rows = jnp.concatenate([step1] * (chunk // d), axis=0)
-    g2, a1 = [], []
+    coef_of(3, 1, flying, step1)
+    x3 = exchange(3)
+
     for h in range(2):
-        g2.append(g1[h] - step_rows * grad_end(1, h, s1))
-        a1.append(gather_start(1, h, g2[h]))
-    x2.wait_send()
-    for sent in s1:
-        sent.wait_send()
-    q0.wait_send()
-    p0.wait_send()
-    coef_of(3, 1, a1)
-    x3 = exchange(3)
-
-    for h in range(2):
-        one, two = gathered(0, h).astype(f32), gathered(1, h).astype(f32)
+        one, two = g_ref[0, h], g_ref[1, h]
         for j in range(own_cols):
             x_v[:, j * patch + h * part : j * patch + (h + 1) * part] = jnp.concatenate(
                 [one[j * d : (j + 1) * d], two[j * d : (j + 1) * d]], axis=0
@@ -299,7 +291,7 @@
     z = over_row(z_buf, z_buf, z_ss, z_rs, shared=True)
     x3.wait_recv()
     image2 = image_of(3)
-    q1 = squares_out(1, g2, image2)
+    q1 = squares_out(1, image2)
 
     z.wait_recv()
     fields = [z_buf[r].astype(f32) for r in range(nr)]
@@ -320,7 +312,8 @@
     ev.start()
     p1 = squares_on(1, q1)
     x3.wait_send()
-    for sent in a1:
+    p0.wait_send()
+    for sent in s1:
         sent.wait_send()
     z.wait_send()
     q1.wait_send()
@@ -332,7 +325,7 @@
     step2 = squares_in(1, p1)
     resid_ref[...] = rhs - step1 * image1 - step2 * image2
     for h in range(2):
-        one, two = gathered(0, h).astype(f32), gathered(1, h).astype(f32)
+        one, two = g_ref[0, h], g_ref[1, h]
         for j in range(own_cols):
             dens_ref[:, j * patch + h * part : j * patch + (h + 1) * part] = (
                 step1 * one[j * d : (j + 1) * d] + step2 * two[j * d : (j + 1) * d]
@@ -369,12 +362,12 @@
     assert block_count == 2 and recv_total == nr * nc and unknowns == own_cols * patch
     slots = own_cols * slot_count
     rows = own_cols * dens_count
-    chunk = rows // nr
     part = patch // 2
+    stages = nr.bit_length() - 1
+    assert nr == 1 << stages
     half = -(-slots // (2 * LANES)) * LANES
     bf = jnp.bfloat16
     f32 = jnp.float32
-    wire = bf if chunk % 16 == 0 else f32
     dma = pltpu.SemaphoreType.DMA
     pair = 2 if nc % 2 == 0 else 1
     u = u_factors.reshape(nc * slots, patch)
@@ -391,13 +384,12 @@
         pltpu.VMEM(far_blocks.shape, bf),
         pltpu.VMEM((2 * dens_count, unknowns), bf),
         pltpu.VMEM((nc // pair, pair * slots), f32),
-        pltpu.VMEM((2, nr, chunk, part), f32),
+        pltpu.VMEM((2, 2, rows, part), f32),
         pltpu.VMEM((2 * dens_count, patch), f32),
         pltpu.VMEM((4, nc, 2 * dens_count, half), bf),
         pltpu.VMEM((4, nc, 2 * dens_count, half), bf),
-        pltpu.VMEM((2, 2, nr, chunk, part), wire),
-        pltpu.VMEM((2, 2, nr, chunk, part), wire),
-        pltpu.VMEM((2, 2, nr, chunk, part), wire),
+        pltpu.VMEM((2, 2, stages, rows, part), bf),
+        pltpu.VMEM((2, 2, stages, rows, part), bf),
         pltpu.VMEM((2, nc, dens_count, LANES), f32),
         pltpu.VMEM((2, nr, dens_count, LANES), f32),
         pltpu.VMEM((nr, 2 * dens_count, patch), bf),
@@ -407,8 +399,7 @@
         pltpu.VMEM((2, 2 * dens_count, patch), bf),
         dma((4,)), dma((nc // pair,)), dma((nc // pair,)), dma((4,)),
         dma((4,)), dma((4,)),
-        dma((2, 2)), dma((2, 2)),
-        dma((2, 2)), dma((2, 2)),
+        dma((2, 2, stages)), dma((2, 2, stages)),
         dma((2,)), dma((2,)),
         dma((2,)), dma((2,)),
         dma, dma,

time: 50.5 us -> 48.8 us (0.966)
  Pallas kernels: 49.7 us -> 48 us
    pallas_call x1, Pallas kernels: 48.1 us -> 46.5 us  [per_device(): pl.pallas_call(functools.partial(kernel, nr, nc, dens_count, own_cols, sl...]
where the time goes in v5:
time: 48.8 us; the launch traced here: 48.7 us
  Pallas kernels  48 us (98%)
  between operations  0.64 us (1%)
    pallas_call x1, Pallas kernels, per_device(): pl.pallas_call(functools.partial(kernel, nr, nc, dens_count, own_cols, sl...  46.5 us
    pallas_call x1, Pallas kernels, per_device(): pl.pallas_call(hand_on, out_shape=tuple((jax.ShapeDtypeStruct(x.shape, x....  1.59 us

profile of v5, /device:TPU:0, one launch (start us, length us, event | category | flops | bytes accessed | tf_op | source)
XLA Modules:
  0.0 48.7 jit_solution(16649657191545457323)
XLA Ops:
  0.6 46.5 %shard_map.94 = (f32[8,4096]{1,0:T(8,128)}, f32[8,512]{1,0:T(8,128)}, f32[1,4096]{1,0:T(1,128)}) custom-call(f32[8,512]{1,0:T(8,128)} %rhs_hbm.1, s32[8,8]{1,0:T(8,128)} %ranks_hbm.1, s32[8,8]{1,0:T(8,128)} %target_hbm.1, s32[32]{0:T(128)} %order_hbm.1, bf16[3072,512]{1,0:T(8,128)(2,1)} %bitcast.2, bf16[3072,512]{1,0:T(8,128)(2,1)} %bitcast.3, ...), custom_call_target="tpu_custom_call" | custom-call | flops 268435456 | bytes 14680064 | tf_op jit(solution)/shard_map/pallas_call | solution.py:410
  47.1 1.6 %shard_map.95 = (f32[8,4096]{1,0:T(8,128)}, f32[8,512]{1,0:T(8,128)}, f32[1,4096]{1,0:T(1,128)}) custom-call(f32[8,4096]{1,0:T(8,128)} %get-tuple-element.6.refs_0_, f32[8,512]{1,0:T(8,128)} %get-tuple-element.7.refs_1_, f32[1,4096]{1,0:T(1,128)} %get-tuple-element.8.refs_2_), custom_call_target="tpu_custom_call" | custom-call | tf_op jit(solution)/shard_map/pallas_call | solution.py:428

commit v6 on v5

--- a/solution.py
+++ b/solution.py
@@ -60,10 +60,11 @@
         )
     ]
     u_copies, v_copies = [], []
-    for q in range(groups):
-        at = slice(q * wide, (q + 1) * wide)
-        u_copies.append(pltpu.make_async_copy(u_hbm.at[at], u_v.at[at], u_sem.at[q]))
-        v_copies.append(pltpu.make_async_copy(v_hbm.at[at], v_v.at[at], v_sem.at[q]))
+    order = [partner_of(my_c // pair, k, groups) for k in range(groups - 1, -1, -1)]
+    for n in range(groups):
+        at = pl.ds(pl.multiple_of(order[n] * wide, wide), wide)
+        u_copies.append(pltpu.make_async_copy(u_hbm.at[at], u_v.at[at], u_sem.at[n]))
+        v_copies.append(pltpu.make_async_copy(v_hbm.at[at], v_v.at[at], v_sem.at[n]))
     f_copies = []
     for b in range(2):
         for h in range(2):
@@ -118,19 +119,35 @@
     def got(rnd, q):
         return jnp.concatenate([unpack(a2a_in[rnd, q * pair + n]) for n in range(pair)], axis=1)
 
-    def exchange(rnd):
-        sent = over_col(a2a_out.at[rnd], a2a_in.at[rnd], a2a_ss.at[rnd], a2a_rs.at[rnd])
+    def post(rnd, n):
+        if n < groups - 1:
+            peers = [order[n] * pair + m for m in range(pair)]
+        else:
+            peers = [my_c // pair * pair + (my_c + m) % pair for m in range(1, pair)]
+        for to in peers:
+            remote(
+                a2a_out.at[rnd, to], a2a_in.at[rnd, my_c], a2a_ss.at[rnd], a2a_rs.at[rnd], my_r, to
+            ).start()
+
+    def posted(rnd):
         a2a_in[rnd, my_c] = a2a_out[rnd, my_c]
-        return sent
+        return remote(
+            a2a_out.at[rnd, : nc - 1], a2a_in.at[rnd, : nc - 1], a2a_ss.at[rnd],
+            a2a_rs.at[rnd], my_r, my_c,
+        )
 
     def back_of(rnd, r, first):
         rb = r.astype(bf)
-        for q in range(groups):
+        for n in range(groups):
             if first:
-                u_copies[q].wait()
-                v_copies[q].start()
-            u = u_v[q * wide : (q + 1) * wide, :]
-            put(rnd, q, lax.dot_general(rb, u, NT, preferred_element_type=f32))
+                u_copies[n].wait()
+                v_copies[n].start()
+            u = u_v[pl.ds(pl.multiple_of(order[n] * wide, wide), wide), :]
+            put(rnd, order[n], lax.dot_general(rb, u, NT, preferred_element_type=f32))
+            if first and n == 0:
+                pl.semaphore_wait(barrier, nc - 1 + nr - 1)
+            post(rnd, n)
+        return posted(rnd)
 
     def image_of(rnd):
         image = jnp.zeros((d, patch), f32)
@@ -185,13 +202,16 @@
                 g = g_ref[0, h] - jnp.concatenate([step] * own_cols, axis=0) * g
             g_ref[it, h] = g
             g = g.astype(bf)
-            for q in range(groups):
-                v = v_v[q * wide : (q + 1) * wide, h * part : (h + 1) * part]
+            for n in range(groups):
+                at = pl.ds(pl.multiple_of(order[n] * wide, wide), wide)
+                v = v_v[at, h * part : (h + 1) * part]
                 full = lax.dot_general(g, v, NT, preferred_element_type=f32) * diag
                 for j in range(own_cols):
-                    parts[q] = parts[q] + full[j * d : (j + 1) * d]
-        for q in range(groups):
-            put(rnd, q, parts[q] * kept_ref[q : q + 1, :])
+                    parts[n] = parts[n] + full[j * d : (j + 1) * d]
+                if h == 1:
+                    put(rnd, order[n], parts[n] * kept_ref[pl.ds(order[n], 1), :])
+                    post(rnd, n)
+        return posted(rnd)
 
     lane = lax.broadcasted_iota(jnp.int32, (d, LANES), 1)
 
@@ -237,9 +257,7 @@
         kept_ref[c // pair : c // pair + 1, at] = kept[c : c + 1]
     small[0].wait()
     rhs = rhs_ref[...]
-    back_of(0, rhs, True)
-    pl.semaphore_wait(barrier, nc - 1 + nr - 1)
-    x0 = exchange(0)
+    x0 = back_of(0, rhs, True)
     for copy in v_copies:
         copy.wait()
     for copy in f_copies[2:] + f_copies[:2]:
@@ -248,14 +266,12 @@
     s0 = grad_start(0, 0)
     x0.wait_send()
     flying, s0 = grad_on(0, s0)
-    coef_of(1, 0, flying, None)
-    x1 = exchange(1)
+    x1 = coef_of(1, 0, flying, None)
     for sent in s0:
         sent.wait_send()
     x1.wait_recv()
     image1 = image_of(1)
-    back_of(2, image1, False)
-    x2 = exchange(2)
+    x2 = back_of(2, image1, False)
     q0 = squares_out(0, image1)
     x1.wait_send()
     x2.wait_recv()
@@ -266,8 +282,7 @@
     x2.wait_send()
     q0.wait_send()
     step1 = squares_in(0, p0)
-    coef_of(3, 1, flying, step1)
-    x3 = exchange(3)
+    x3 = coef_of(3, 1, flying, step1)
 
     for h in range(2):
         one, two = g_ref[0, h], g_ref[1, h]

time: 48.8 us -> 48.6 us (level)
  no operation moved by 1% of the time
where the time goes in v6:
time: 48.6 us; the launch traced here: 48.4 us
  Pallas kernels  47.8 us (98%)
  between operations  0.64 us (1%)
    pallas_call x1, Pallas kernels, per_device(): pl.pallas_call(functools.partial(kernel, nr, nc, dens_count, own_cols, sl...  46.2 us
    pallas_call x1, Pallas kernels, per_device(): pl.pallas_call(hand_on, out_shape=tuple((jax.ShapeDtypeStruct(x.shape, x....  1.59 us

profile of v6, /device:TPU:0, one launch (start us, length us, event | category | flops | bytes accessed | tf_op | source)
XLA Modules:
  0.0 48.4 jit_solution(11210503859966301587)
XLA Ops:
  0.6 46.2 %shard_map.94 = (f32[8,4096]{1,0:T(8,128)}, f32[8,512]{1,0:T(8,128)}, f32[1,4096]{1,0:T(1,128)}) custom-call(f32[8,512]{1,0:T(8,128)} %rhs_hbm.1, s32[8,8]{1,0:T(8,128)} %ranks_hbm.1, s32[8,8]{1,0:T(8,128)} %target_hbm.1, s32[32]{0:T(128)} %order_hbm.1, bf16[3072,512]{1,0:T(8,128)(2,1)} %bitcast.2, bf16[3072,512]{1,0:T(8,128)(2,1)} %bitcast.3, ...), custom_call_target="tpu_custom_call" | custom-call | flops 268435456 | bytes 14680064 | tf_op jit(solution)/shard_map/pallas_call | solution.py:425
  46.8 1.6 %shard_map.95 = (f32[8,4096]{1,0:T(8,128)}, f32[8,512]{1,0:T(8,128)}, f32[1,4096]{1,0:T(1,128)}) custom-call(f32[8,4096]{1,0:T(8,128)} %get-tuple-element.6.refs_0_, f32[8,512]{1,0:T(8,128)} %get-tuple-element.7.refs_1_, f32[1,4096]{1,0:T(1,128)} %get-tuple-element.8.refs_2_), custom_call_target="tpu_custom_call" | custom-call | tf_op jit(solution)/shard_map/pallas_call | solution.py:443

commit v7 on v6

--- a/solution.py
+++ b/solution.py
@@ -292,13 +292,8 @@
             ).astype(bf)
 
     def field_of(b):
-        field = jnp.zeros((2 * d, patch), f32)
-        for j in range(own_cols):
-            at = slice(j * patch, (j + 1) * patch)
-            field = field + lax.dot_general(
-                x_v[:, at], f_v[b, :, at], NT, preferred_element_type=f32
-            )
-        return field.astype(bf)
+        field = lax.dot_general(f_v[b], x_v[...], NT, preferred_element_type=f32)
+        return field.T.astype(bf)
 
     for copy in f_copies + small[2:]:
         copy.wait()

time: 48.6 us -> 50.5 us (1.039)
  Pallas kernels: 47.8 us -> 49.6 us
    pallas_call x1, Pallas kernels: 46.2 us -> 48 us  [per_device(): pl.pallas_call(functools.partial(kernel, nr, nc, dens_count, own_cols, sl...]
where the time goes in v7:
time: 50.5 us; the launch traced here: 50.3 us
  Pallas kernels  49.6 us (98%)
  between operations  0.64 us (1%)
    pallas_call x1, Pallas kernels, per_device(): pl.pallas_call(functools.partial(kernel, nr, nc, dens_count, own_cols, sl...  48 us
    pallas_call x1, Pallas kernels, per_device(): pl.pallas_call(hand_on, out_shape=tuple((jax.ShapeDtypeStruct(x.shape, x....  1.59 us

profile of v7, /device:TPU:0, one launch (start us, length us, event | category | flops | bytes accessed | tf_op | source)
XLA Modules:
  0.0 50.3 jit_solution(3389299205619231102)
XLA Ops:
  0.6 48.0 %shard_map.94 = (f32[8,4096]{1,0:T(8,128)}, f32[8,512]{1,0:T(8,128)}, f32[1,4096]{1,0:T(1,128)}) custom-call(f32[8,512]{1,0:T(8,128)} %rhs_hbm.1, s32[8,8]{1,0:T(8,128)} %ranks_hbm.1, s32[8,8]{1,0:T(8,128)} %target_hbm.1, s32[32]{0:T(128)} %order_hbm.1, bf16[3072,512]{1,0:T(8,128)(2,1)} %bitcast.2, bf16[3072,512]{1,0:T(8,128)(2,1)} %bitcast.3, ...), custom_call_target="tpu_custom_call" | custom-call | flops 268435456 | bytes 14680064 | tf_op jit(solution)/shard_map/pallas_call | solution.py:420
  48.7 1.6 %shard_map.95 = (f32[8,4096]{1,0:T(8,128)}, f32[8,512]{1,0:T(8,128)}, f32[1,4096]{1,0:T(1,128)}) custom-call(f32[8,4096]{1,0:T(8,128)} %get-tuple-element.6.refs_0_, f32[8,512]{1,0:T(8,128)} %get-tuple-element.7.refs_1_, f32[1,4096]{1,0:T(1,128)} %get-tuple-element.8.refs_2_), custom_call_target="tpu_custom_call" | custom-call | tf_op jit(solution)/shard_map/pallas_call | solution.py:438

commit v8 on v6

--- a/solution.py
+++ b/solution.py
@@ -291,18 +291,18 @@
                 [one[j * d : (j + 1) * d], two[j * d : (j + 1) * d]], axis=0
             ).astype(bf)
 
-    def field_of(b):
-        field = jnp.zeros((2 * d, patch), f32)
-        for j in range(own_cols):
+    def field_of(b, field, cols):
+        for j in cols:
             at = slice(j * patch, (j + 1) * patch)
             field = field + lax.dot_general(
                 x_v[:, at], f_v[b, :, at], NT, preferred_element_type=f32
             )
-        return field.astype(bf)
+        return field
 
     for copy in f_copies + small[2:]:
         copy.wait()
-    z_buf[my_r] = field_of(1)
+    no_field = jnp.zeros((2 * d, patch), f32)
+    z_buf[my_r] = field_of(1, no_field, range(own_cols)).astype(bf)
     z = over_row(z_buf, z_buf, z_ss, z_rs, shared=True)
     x3.wait_recv()
     image2 = image_of(3)
@@ -320,12 +320,14 @@
     fc = over_col(fc_out, fc_in, fc_ss, fc_rs)
     fc_in[my_c] = fc_out[my_c]
 
-    ev_out[...] = field_of(0)
+    even = field_of(0, no_field, range(own_cols // 2))
+    p1 = squares_on(1, q1)
+    even = field_of(0, even, range(own_cols // 2, own_cols))
+    ev_out[...] = even.astype(bf)
     odd = my_c % 2
     ev_row = (1 - odd) * ((my_r + nr // 2) % nr) + odd * my_r
     ev = remote(ev_out, ev_in.at[odd], ev_ss, ev_rs.at[odd], ev_row, my_c - odd)
     ev.start()
-    p1 = squares_on(1, q1)
     x3.wait_send()
     p0.wait_send()
     for sent in s1:

time: 48.6 us -> 48 us (0.988)
  Pallas kernels: 47.8 us -> 47.2 us
    pallas_call x1, Pallas kernels: 46.2 us -> 45.6 us  [per_device(): pl.pallas_call(functools.partial(kernel, nr, nc, dens_count, own_cols, sl...]
where the time goes in v8:
time: 48 us; the launch traced here: 47.8 us
  Pallas kernels  47.2 us (98%)
  between operations  0.64 us (1%)
    pallas_call x1, Pallas kernels, per_device(): pl.pallas_call(functools.partial(kernel, nr, nc, dens_count, own_cols, sl...  45.6 us
    pallas_call x1, Pallas kernels, per_device(): pl.pallas_call(hand_on, out_shape=tuple((jax.ShapeDtypeStruct(x.shape, x....  1.59 us

profile of v8, /device:TPU:0, one launch (start us, length us, event | category | flops | bytes accessed | tf_op | source)
XLA Modules:
  0.0 47.8 jit_solution(15701106610646202713)
XLA Ops:
  0.6 45.6 %shard_map.94 = (f32[8,4096]{1,0:T(8,128)}, f32[8,512]{1,0:T(8,128)}, f32[1,4096]{1,0:T(1,128)}) custom-call(f32[8,512]{1,0:T(8,128)} %rhs_hbm.1, s32[8,8]{1,0:T(8,128)} %ranks_hbm.1, s32[8,8]{1,0:T(8,128)} %target_hbm.1, s32[32]{0:T(128)} %order_hbm.1, bf16[3072,512]{1,0:T(8,128)(2,1)} %bitcast.2, bf16[3072,512]{1,0:T(8,128)(2,1)} %bitcast.3, ...), custom_call_target="tpu_custom_call" | custom-call | flops 268435456 | bytes 14680064 | tf_op jit(solution)/shard_map/pallas_call | solution.py:427
  46.2 1.6 %shard_map.95 = (f32[8,4096]{1,0:T(8,128)}, f32[8,512]{1,0:T(8,128)}, f32[1,4096]{1,0:T(1,128)}) custom-call(f32[8,4096]{1,0:T(8,128)} %get-tuple-element.6.refs_0_, f32[8,512]{1,0:T(8,128)} %get-tuple-element.7.refs_1_, f32[1,4096]{1,0:T(1,128)} %get-tuple-element.8.refs_2_), custom_call_target="tpu_custom_call" | custom-call | tf_op jit(solution)/shard_map/pallas_call | solution.py:445
